TPU v7x, 256 devices: a whole 4x4x8 slice. The times are simulated.
256 devices in a mesh: layer: 32 (over x, y, core), feat: 8 (over z).
Axes of the slice: x: 4, y: 4, z: 8, core: 2. Of those that a mesh axis runs over, the one named last changes fastest.
Arguments:
- cotangent: bfloat16 [2, 1024, 5120], P(None, 'layer', 'feat'), may hold values from -6 to 6
- decoder: bfloat16 [65536, 2, 5120], P(('layer', 'feat')), may hold values from -0.0625 to 0.0625
- encoder: bfloat16 [5120, 65536], P(None, ('layer', 'feat')), may hold values from -0.375 to 0.375
- preact: bfloat16 [1024, 65536], P(None, ('layer', 'feat')), may hold values from -6 to 6
- block_ids: int32 [2, 16, 32], replicated, may hold values from 0 to 255, as said below
- block_counts: int32 [2, 16], replicated, may hold values from 8 to 32, as said below
Outputs:
- feature_grad: bfloat16 [1024, 65536], P(None, ('layer', 'feat'))
- input_grad: bfloat16 [2, 1024, 5120], P(None, 'layer', 'feat')
Inputs may be any that keep to these rules, and one draw needn't show every extreme that they name: `block_ids`: within one list the entries are distinct block numbers; entries past the count are valid numbers and are ignored. `block_counts`: the count 32 is reached by some list in every draw.
All inputs are finite; a program needn't handle non-finite values.
Results may differ from a plain program's by a relative error of at most 0.005.
Values may be sent and summed in bfloat16 or wider, within the bound.
A program may use at most 128 MiB of HBM per device.

v0:
```python
import jax
import jax.numpy as jnp
from jax import lax
from jax.sharding import PartitionSpec as P

WIN = 64


def body(cotangent, decoder, encoder, preact, block_ids, block_counts):
    layer_devices = lax.axis_size("layer")
    feat_devices = lax.axis_size("feat")
    num_layers = decoder.shape[1]
    groups = layer_devices // num_layers
    feat_dev = decoder.shape[0]
    width = decoder.shape[2]
    tokens = preact.shape[0]
    windows = tokens // WIN
    local_blocks = feat_dev // 128
    layer_index = lax.axis_index("layer")
    feat_index = lax.axis_index("feat")
    source = layer_index // groups
    slot_index = layer_index % groups * feat_devices + feat_index
    first_block = slot_index * local_blocks
    block_list = lax.dynamic_index_in_dim(block_ids, source, 0, keepdims=False)
    count_list = lax.dynamic_index_in_dim(block_counts, source, 0, keepdims=False)
    live_slots = jnp.arange(block_list.shape[1])[None, :] < count_list[:, None]
    own_blocks = first_block + jnp.arange(local_blocks)
    blockhit = jnp.any(
        (block_list[:, :, None] == own_blocks[None, None, :]) & live_slots[:, :, None], axis=1
    )
    spread = jnp.broadcast_to(blockhit[:, None, :, None], (windows, WIN, local_blocks, 128))
    active = spread.reshape(tokens, feat_dev) & (preact > 0)
    wide_rows = lax.all_gather(cotangent, "feat", axis=2, tiled=True)
    piece = lax.all_gather(wide_rows, "layer", axis=1, tiled=True)

    def add_target(target, total):
        cot_rows = lax.dynamic_index_in_dim(piece, target, 0, keepdims=False)
        weights = lax.dynamic_index_in_dim(decoder, target, 1, keepdims=False)
        return total + lax.dot_general(
            cot_rows, weights, (((1,), (1,)), ((), ())), preferred_element_type=jnp.float32
        )

    act_grad = lax.fori_loop(
        source, num_layers, add_target, jnp.zeros((piece.shape[1], feat_dev), jnp.float32)
    )
    feature_grad = jnp.where(active, act_grad, 0.0).astype(jnp.bfloat16)
    slice_width = width // feat_devices
    partial_t = lax.psum_scatter(
        lax.dot_general(
            encoder, feature_grad, (((1,), (1,)), ((), ())), preferred_element_type=jnp.float32
        ),
        "feat",
        scatter_dimension=0,
        tiled=True,
    )
    received = lax.all_to_all(partial_t, "layer", split_axis=1, concat_axis=0, tiled=True)
    token_share = tokens // layer_devices
    summed = received.reshape(num_layers, groups, slice_width, token_share).sum(axis=1)
    input_grad = jnp.transpose(summed, (0, 2, 1)).astype(jnp.bfloat16)
    return (feature_grad, input_grad)


def solution(mesh):
    return jax.shard_map(
        body,
        mesh=mesh,
        in_specs=(
            P(None, "layer", "feat"),
            P(("layer", "feat"), None, None),
            P(None, ("layer", "feat")),
            P(None, ("layer", "feat")),
            P(),
            P(),
        ),
        out_specs=(P(None, ("layer", "feat")), P(None, "layer", "feat")),
        check_vma=False,
    )
```

profile of v0, /device:TPU:4, one launch (start us, length us, event | category | flops | bytes accessed | tf_op | source)
XLA Modules:
  0.0 416.7 jit_solution(8372943590065807268)
XLA Ops:
  7.2 0.0 copy-start
  7.2 0.0 all-gather.2.cloned.1.call-start
  7.2 31.7 %all_gather.6 = bf16[2,32,5120]{2,1,0:T(8,128)(2,1)} all-gather(bf16[2,32,640]{2,1,0:T(8,128)(2,1)} %param.8), channel_id=1, replica_groups=mesh['layer'=32,'feat'=8] {'feat'}, dimensions={2}, use_global_device_ids=true | all-gather | bytes 737280 | tf_op jit(solution)/shard_map/all_gather | solution.py:33
  38.9 0.0 all-gather.2.cloned.1.call-update
  38.9 0.0 reduce-scatter.2.cloned.1.call-start
  39.0 0.0 copy-start.2
  39.0 0.0 copy-start.1
  39.0 6.1 %copy.15 = bf16[256,2,5120]{2,0,1:T(8,128)(2,1)} copy(bf16[256,2,5120]{2,1,0:T(2,128)(2,1)} %param.9) | data formatting | bytes 10485760 | tf_op jit(solution)/shard_map/while | solution.py:43
  45.1 0.0 copy-done.2
  45.2 0.0 copy-done.1
  45.2 0.1 iota_compare_fusion
  45.3 0.2 and_reduce_fusion
  45.4 0.2 broadcast_in_dim.5
  45.7 0.8 reshape.46
  46.4 2.1 copy.13
  48.5 77.2 %all-gather.2.cloned.1.call-done = bf16[2,1024,5120]{2,1,0:T(8,128)(2,1)} async-done(((bf16[2,32,5120]{2,1,0:T(8,128)(2,1)}), bf16[2,1024,5120]{2,1,0:T(8,128)(2,1)}) %all-gather.2.cloned.1.call-update) | async-done | bytes 20971536 | tf_op jit(solution)/shard_map/all_gather | solution.py:34
  125.7 1.0 broadcast_in_dim.6.clone
  126.7 8.9 %while.10 = (s32[]{:T(128)}, f32[1024,256]{1,0:T(8,128)}, bf16[2,1024,5120]{2,1,0:T(8,128)(2,1)}, bf16[256,2,5120]{2,0,1:T(8,128)(2,1)}, s32[]{:T(128)}, /*index=5*/s32[]{:T(128)}, s32[]{:T(128)}) while((s32[]{:T(128)}, f32[1024,256]{1,0:T(8,128)}, bf16[2,1024,5120]{2,1,0:T(8,128)(2,1)}, bf16[256,2,5120]{2,0,1:T(8,128)(2,1)}, s32[]{:T(128)}, ...), condition=%wide.region_2.3_spmd, body=%wide.region_1.2_spmd.sunk | while | flops 2684616704 | bytes 15205487 | solution.py:43
  126.7 8.8 %fusion.18 = f32[1024,256]{1,0:T(8,128)} fusion(f32[1024,256]{1,0:T(8,128)} %get-tuple-element.78, bf16[256,2,5120]{2,0,1:T(8,128)(2,1)} %get-tuple-element.87, s32[]{:T(128)S(6)} %select_n.33, bf16[2,1024,5120]{2,1,0:T(8,128)(2,1)} %get-tuple-element.86), kind=kOutput, calls=%fused_computation.5.clone.1 | convolution fusion | flops 2684616704 | bytes 15205376 | tf_op jit(solution)/shard_map/while/body/dot_general | solution.py:39
  135.6 2.2 copy.16
  137.8 1.5 select_convert_fusion
  139.3 0.0 copy-done
  139.3 8.6 %convolution_bitcast_fusion = f32[5120,1024]{0,1:T(8,128)} fusion(bf16[1024,256]{0,1:T(8,128)(2,1)S(1)} %select_convert_fusion, bf16[5120,256]{1,0:T(8,128)(2,1)S(1)} %copy-done), kind=kOutput, calls=%fused_computation.7 | convolution fusion | flops 2684354560 | bytes 24117248 | tf_op jit(solution)/shard_map/dot_general | solution.py:49
  147.9 0.0 reduce-scatter.2.cloned.1.call-update
  147.9 220.5 %reduce-scatter.2.cloned.1.call-done = f32[640,1024]{0,1:T(8,128)} async-done(((f32[5120,1024]{0,1:T(8,128)}), f32[640,1024]{0,1:T(8,128)}) %reduce-scatter.2.cloned.1.call-update) | async-done | bytes 2621456 | tf_op jit(solution)/shard_map/reduce_scatter | solution.py:48
  368.4 7.5 %all-to-all-start = ((f32[640,32,32]{0,2,1:T(8,128)}), f32[640,32,32]{0,2,1:T(8,128)}, u32[]{:S(2)}, u32[]{:S(2)}) async-start(f32[640,32,32]{0,2,1:T(8,128)} %bitcast.34), calls=%async_computation.1 | async-start | bytes 5242880 | tf_op jit(solution)/shard_map/all_to_all | solution.py:56
  375.8 1.0 copy.17
  376.8 30.5 %all-to-all-done = f32[640,32,32]{0,2,1:T(8,128)} async-done(((f32[640,32,32]{0,2,1:T(8,128)}), f32[640,32,32]{0,2,1:T(8,128)}, u32[]{:S(2)}, u32[]{:S(2)}) %all-to-all-start) | async-done | bytes 2621472 | tf_op jit(solution)/shard_map/all_to_all | solution.py:56
  407.3 2.5 bitcast_reduce_fusion
  (3 shorter events, 0.0 us)
Async XLA Ops:
  7.2 132.1 %copy-start = (bf16[5120,256]{1,0:T(8,128)(2,1)S(1)}, bf16[5120,256]{1,0:T(8,128)(2,1)}, u32[]{:S(2)}) copy-start(bf16[5120,256]{1,0:T(8,128)(2,1)} %param.10) | copy-start | bytes 7864324
  7.2 118.5 %all-gather.2.cloned.1.call-start = ((), (), s32[]{:S(2)}) async-start(), calls=%async_computation.2 | async-start | bytes 21626880 | tf_op jit(solution)/shard_map/all_gather | solution.py:34
  38.9 329.4 %reduce-scatter.2.cloned.1.call-start = ((), (), s32[]{:S(2)}) async-start(), calls=%async_computation.3 | async-start | bytes 23592960 | tf_op jit(solution)/shard_map/reduce_scatter | solution.py:48
  39.0 6.1 %copy-start.2 = (s32[2,16]{1,0:T(2,128)S(1)}, s32[2,16]{1,0:T(2,128)}, u32[]{:S(2)}) copy-start(s32[2,16]{1,0:T(2,128)} %param.13) | copy-start | bytes 388
  39.0 6.1 %copy-start.1 = (s32[2,16,32]{2,1,0:T(8,128)S(1)}, s32[2,16,32]{2,1,0:T(8,128)}, u32[]{:S(2)}) copy-start(s32[2,16,32]{2,1,0:T(8,128)} %param.12) | copy-start | bytes 12292
  368.4 39.0 %all-to-all-start = ((f32[640,32,32]{0,2,1:T(8,128)}), f32[640,32,32]{0,2,1:T(8,128)}, u32[]{:S(2)}, u32[]{:S(2)}) async-start(f32[640,32,32]{0,2,1:T(8,128)} %bitcast.34), calls=%async_computation.1 | async-start | bytes 5242880 | tf_op jit(solution)/shard_map/all_to_all | solution.py:56
Sparse Core Ops, SparseCore 0:
  39.1 86.5 all-gather.1
  148.0 220.2 reduce-scatter.1
where the time goes:
time: 420 us; the launch traced here: 417 us
  waiting for transfers between devices  328 us (78%)
  blocking collectives  31.7 us (8%)
  matrix products  17.5 us (4%)
  between operations  14.1 us (3%)
  local copies, waits for them, and re-layouts  13.4 us (3%)
  starting transfers between devices  7.54 us (2%)
  other arithmetic  4.28 us (1%)
    reduce_scatter x1, waiting for transfers between devices, body(): lax.psum_scatter(lax.dot_general(encoder, feature_grad, (((1,), (1,)), ((...  220 us
    all_gather x1, waiting for transfers between devices, body(): piece = lax.all_gather(wide_rows, 'layer', axis=1, tiled=True)  77.2 us
    all_gather x1, blocking collectives, body(): wide_rows = lax.all_gather(cotangent, 'feat', axis=2, tiled=True)  31.7 us
    all_to_all x1, waiting for transfers between devices, body(): lax.all_to_all(partial_t, 'layer', split_axis=1, concat_axis=0, tiled=True)  30.5 us
    dot_general x1, matrix products, add_target(): lax.dot_general(cot_rows, weights, (((1,), (1,)), ((), ())), preferred_el...  8.85 us
    dot_general x1, matrix products, body(): lax.dot_general(encoder, feature_grad, (((1,), (1,)), ((), ())), preferre...  8.6 us
  transfers between devices with their start and end apart: 3, of which 3 were waited for; matrix products, arithmetic and copies ran while one was open for 3% of the time, Pallas kernels for 0%

commit v1 on v0

v1 whole, which is shorter than its diff:
```python
import functools

import jax
import jax.numpy as jnp
from jax import lax
from jax.experimental import pallas as pl
from jax.experimental.pallas import tpu as pltpu
from jax.sharding import PartitionSpec as P

MESH = pl.DeviceIdType.MESH
WIN = 64
ROWS = WIN // 2
HALF = ROWS // 2
BLOCK = 128
F32 = jnp.float32
BF16 = jnp.bfloat16


class Semaphores:
    def __init__(self, send, recv):
        self.send, self.recv, self.used = send, recv, 0

    def take(self, count=1):
        first = self.used
        self.used += count
        return first

    def copy(self, source, target, index, device):
        return pltpu.make_async_remote_copy(
            src_ref=source,
            dst_ref=target,
            send_sem=self.send.at[index],
            recv_sem=self.recv.at[index],
            device_id=device,
            device_id_type=MESH,
        )


def both(index):
    return pl.ds(index * HALF, HALF)


def ring_gather(sems, n, me, right, left, chunk, subs, drains):
    steps = n // 2
    base = sems.take(steps * 2 * subs)
    sides = ((right, -1), (left, 1))

    def copies(step, sub, sent):
        last = step == steps
        found = []
        for side, (device, sign) in enumerate(sides):
            at = lax.rem(me + (n + sign * (step - (1 if sent else 0))), n)
            rows = both(side) if last else pl.ds(0, ROWS)
            ref = chunk(at, sub, rows)
            found.append(sems.copy(ref, ref, base + ((step - 1) * 2 + side) * subs + sub, device))
        return found

    def over(fn):
        if subs == 1:
            fn(0)
        else:
            def loop(sub, carry):
                fn(sub)
                return carry

            lax.fori_loop(0, subs, loop, 0)

    def stage(step):
        def run():
            def one(sub):
                if step > 1:
                    for copy in copies(step - 1, sub, False):
                        copy.wait_recv()
                if step <= steps:
                    for copy in copies(step, sub, True):
                        copy.start()

            over(one)

        return run

    def drain():
        for step in range(1, steps + 1):
            def one(sub):
                for copy in copies(step, sub, True):
                    copy.wait_send()

            over(one)

    drains.append(drain)
    return [stage(step) for step in range(1, steps + 2)]


def ring_scatter(sems, n, me, right, left, own, outer, inner, bufs, drains):
    half_send, half_recv, full_send, full_recv = bufs
    steps = n // 2
    base = sems.take(steps * 2 * outer)
    sides = ((right, 1), (left, -1))

    def copy_of(step, side, o):
        device = sides[side][0]
        index = base + ((step - 1) * 2 + side) * outer + o
        if step == 1:
            return sems.copy(half_send.at[side, o], half_recv.at[side, o], index, device)
        return sems.copy(full_send.at[step - 2, side, o], full_recv.at[step - 2, side, o], index, device)

    def loop_inner(fn):
        if inner == 1:
            fn(0)
        else:
            def loop(j, carry):
                fn(j)
                return carry

            lax.fori_loop(0, inner, loop, 0)

    def stage(step):
        def one(o, carry):
            for side, (_, sign) in enumerate(sides):
                at = lax.rem(me + (n + sign * (steps - step + 1)), n)
                if step > 1:
                    copy_of(step - 1, side, o).wait_recv()

                def add(j):
                    if step == 1:
                        half_send[side, o, j] = own(at, o, j)[pl.ds(side * HALF, HALF), :].astype(BF16)
                    elif step == 2:
                        mine = pl.ds(side * HALF, HALF)
                        other = pl.ds((1 - side) * HALF, HALF)
                        ref = own(at, o, j)
                        full_send[step - 2, side, o, j, mine, :] = (
                            ref[mine, :] + half_recv[side, o, j].astype(F32)
                        ).astype(BF16)
                        full_send[step - 2, side, o, j, other, :] = ref[other, :].astype(BF16)
                    else:
                        full_send[step - 2, side, o, j] = (
                            own(at, o, j)[...] + full_recv[step - 3, side, o, j].astype(F32)
                        ).astype(BF16)

                loop_inner(add)
                copy_of(step, side, o).start()
            return carry

        return lambda: lax.fori_loop(0, outer, one, 0)

    def final():
        def one(o, carry):
            for side in range(2):
                copy_of(steps, side, o).wait_recv()

            def add(j):
                ref = own(me, o, j)
                if steps == 1:
                    for side in range(2):
                        mine = pl.ds(side * HALF, HALF)
                        ref[mine, :] = ref[mine, :] + half_recv[side, o, j].astype(F32)
                else:
                    ref[...] = (
                        ref[...]
                        + full_recv[steps - 2, 0, o, j].astype(F32)
                        + full_recv[steps - 2, 1, o, j].astype(F32)
                    )

            loop_inner(add)
            return carry

        lax.fori_loop(0, outer, one, 0)

    def drain():
        for step in range(1, steps + 1):
            def one(o, carry):
                for side in range(2):
                    copy_of(step, side, o).wait_send()
                return carry

            lax.fori_loop(0, outer, one, 0)

    drains.append(drain)
    return [stage(step) for step in range(1, steps + 1)] + [final]


def merge(*streams):
    order = []
    for which, (start, pace, stages) in enumerate(streams):
        for k, stage in enumerate(stages):
            order.append((start + pace * k, which, k, stage))
    for _, _, _, stage in sorted(order, key=lambda item: item[:3]):
        stage()


def kernel(dims, cot, dec, enc, pre, hit, fg_out, ig_out, g0, g1, dv, ev, pv, fg, acc, part, xr, bufs, send, recv, local):
    nx, ny, nz, cut, rcut, width = dims
    hx = nx // 2
    layer = lax.axis_index("layer")
    z = lax.axis_index("feat")
    c = lax.rem(layer, 2)
    y = lax.rem(layer // 2, ny)
    x = layer // (2 * ny)
    is_first = x < hx

    def device(x, y, z, c):
        return ((x * ny + y) * 2 + c, z)

    def shifted(at, n, by):
        return lax.rem(at + by, n)

    sibling = device(x, y, z, 1 - c)
    x_peers = [device(shifted(x, nx, k), y, z, c) for k in range(1, nx)]
    x_right, x_left = x_peers[0], x_peers[-1]
    y_right, y_left = device(x, shifted(y, ny, 1), z, c), device(x, shifted(y, ny, ny - 1), z, c)
    z_right, z_left = device(x, y, shifted(z, nz, 1), c), device(x, y, shifted(z, nz, nz - 1), c)
    peers = [sibling] + x_peers + [y_right, y_left, z_right, z_left]

    own_copies = [
        pltpu.make_async_copy(cot.at[0], g0.at[x, y, z], local.at[0]),
        pltpu.make_async_copy(cot.at[1], g1.at[x, y, z], local.at[1]),
    ]
    for copy in own_copies:
        copy.start()

    barrier = pltpu.get_barrier_semaphore()
    for peer in peers:
        pl.semaphore_signal(barrier, inc=1, device_id=peer, device_id_type=MESH)
    weight_copies = [
        pltpu.make_async_copy(dec.at[1], dv.at[1, c], local.at[2]),
        pltpu.make_async_copy(dec.at[0], dv.at[0, c], local.at[3]),
        pltpu.make_async_copy(enc, ev.at[c], local.at[4]),
        pltpu.make_async_copy(pre.at[:, c], pv.at[c], local.at[5]),
    ]
    for copy in own_copies:
        copy.wait()
    pl.semaphore_wait(barrier, len(peers))

    sems = Semaphores(send, recv)
    drains = []

    lo, hi = pl.ds(0, cut), pl.ds(cut, width - cut)
    rlo, rhi = pl.ds(0, rcut), pl.ds(rcut, width - rcut)
    a_base = sems.take(nx - 1)
    t_base = sems.take(nx - 1)

    def x_copy(k, sent, target):
        at = x if sent else shifted(x, nx, nx - k)
        if target:
            ref = g1.at[at, y, z, :, hi]
            return sems.copy(ref, ref, a_base + k - 1, x_peers[k - 1])
        ref = g0.at[at, y, z]
        return sems.copy(ref, ref, t_base + k - 1, x_peers[k - 1])

    def x_start():
        for k in range(1, nx):
            x_copy(k, True, 1).start()
            pl.when(shifted(x, nx, k) < hx)(lambda k=k: x_copy(k, True, 0).start())

    def x_end():
        for k in range(1, nx):
            x_copy(k, False, 1).wait_recv()

        @pl.when(is_first)
        def _():
            for k in range(1, nx):
                x_copy(k, False, 0).wait_recv()

    def x_drain():
        for k in range(1, nx):
            x_copy(k, True, 1).wait_send()
            pl.when(shifted(x, nx, k) < hx)(lambda k=k: x_copy(k, True, 0).wait_send())

    drains.append(x_drain)

    az = ring_gather(sems, nz, z, z_right, z_left, lambda i, s, r: g1.at[x, y, i, r, lo], 1, drains)
    ay = ring_gather(sems, ny, y, y_right, y_left, lambda i, s, r: g1.at[x, i, :, r, lo], 1, drains)
    ax = ring_gather(sems, nx, x, x_right, x_left, lambda i, s, r: g1.at[i, s, :, r, lo], ny, drains)
    bz = ring_gather(sems, nz, z, z_right, z_left, lambda i, s, r: g1.at[:, y, i, r, hi], 1, drains)
    by = ring_gather(sems, ny, y, y_right, y_left, lambda i, s, r: g1.at[s, i, :, r, hi], nx, drains)
    first_drains = []
    dz = ring_gather(sems, nz, z, z_right, z_left, lambda i, s, r: g0.at[:, y, i, r, rlo], 1, first_drains)
    dy = ring_gather(sems, ny, y, y_right, y_left, lambda i, s, r: g0.at[s, i, :, r, rlo], nx, first_drains)
    cy = ring_gather(sems, ny, y, y_right, y_left, lambda i, s, r: g0.at[:, i, z, r, rhi], 1, first_drains)
    cz = ring_gather(sems, nz, z, z_right, z_left, lambda i, s, r: g0.at[s, :, i, r, rhi], nx, first_drains)

    def joined(*rings):
        stages = list(rings[0])
        for ring in rings[1:]:
            end, start = stages.pop(), ring[0]

            def link(end=end, start=start):
                end()
                start()

            stages.append(link)
            stages.extend(ring[1:])
        return stages

    def first_only(stages):
        def wrap(stage):
            return lambda: pl.when(is_first)(lambda: stage())

        return [wrap(stage) for stage in stages]

    dec1 = sems.copy(dec.at[1], dv.at[1, c], sems.take(), sibling)
    dec0 = sems.copy(dec.at[0], dv.at[0, c], sems.take(), sibling)
    enc1 = sems.copy(enc, ev.at[c], sems.take(), sibling)
    pre1 = sems.copy(pre.at[:, 1 - c], pv.at[c], sems.take(), sibling)

    def weights_start():
        weight_copies[0].start()
        dec1.start()

        @pl.when(is_first)
        def _():
            weight_copies[1].start()
            dec0.start()

        for copy in weight_copies[2:] + [enc1, pre1]:
            copy.start()

    merge(
        (0.0, 1.0, joined(az, ay, ax)),
        (0.1, 1.0, [x_start]),
        (0.2, 1.0, [weights_start]),
        (0.9, 1.0, [x_end]),
        (0.95, 1.0, joined(bz, by)),
        (0.96, 1.0, first_only(joined(dz, dy))),
        (0.97, 1.0, first_only(joined(cy, cz))),
    )

    tokens = nx * ny * ROWS
    feats = dv.shape[2]
    contract = (((1,), (1,)), ((), ()))
    weight_copies[0].wait()
    dec1.wait_recv()

    @pl.when(is_first)
    def _():
        weight_copies[1].wait()
        dec0.wait_recv()

    acc[...] = jnp.zeros_like(acc)

    def act_step(zz, carry):
        columns = pl.ds(pl.multiple_of(zz * width, 128), width)
        rows1 = g1[:, :, zz].reshape(tokens, width)
        for side in range(2):
            acc[side] += lax.dot_general(rows1, dv[1, side, :, columns], contract, preferred_element_type=F32)

        @pl.when(is_first)
        def _():
            rows0 = g0[:, :, zz].reshape(tokens, width)
            for side in range(2):
                acc[side] += lax.dot_general(rows0, dv[0, side, :, columns], contract, preferred_element_type=F32)

        return carry

    lax.fori_loop(0, nz, act_step, 0)
    weight_copies[3].wait()
    pre1.wait_recv()

    def mask_step(w, carry):
        for side in range(2):
            live = (pv[side, w].astype(F32) > 0.0) & (hit[w, :, pl.ds(side * feats, feats)] > 0.0)
            grad = jnp.where(live, acc[side, pl.ds(pl.multiple_of(w * ROWS, ROWS), ROWS), :], 0.0)
            fg[side, w] = grad.astype(BF16)
        return carry

    lax.fori_loop(0, nx * ny, mask_step, 0)
    fg_local = pltpu.make_async_copy(fg.at[c], fg_out.at[:, c], local.at[6])
    fg_index = sems.take()
    fg_remote = sems.copy(fg.at[1 - c], fg_out.at[:, c], fg_index, sibling)
    fg_local.start()
    fg_remote.start()
    weight_copies[2].wait()
    enc1.wait_recv()

    def part_step(zz, carry):
        at = pl.ds(pl.multiple_of(zz * width, 128), width)
        total = None
        for side in range(2):
            term = lax.dot_general(
                fg[side].reshape(tokens, feats), ev[side, at, :], contract, preferred_element_type=F32
            )
            total = term if total is None else total + term
        part[:, :, zz] = total.reshape(nx, ny, ROWS, width)
        return carry

    lax.fori_loop(0, nz, part_step, 0)

    ylo, zhi = pl.ds(0, rcut + 128), pl.ds(rcut + 128, width - rcut - 128)
    y1 = ring_scatter(
        sems, ny, y, y_right, y_left, lambda i, o, j: part.at[o, i, j, :, ylo], nx, nz, bufs[0:4], drains
    )
    z1 = ring_scatter(
        sems, nz, z, z_right, z_left, lambda i, o, j: part.at[o, j, i, :, zhi], nx, ny, bufs[4:8], drains
    )
    z2 = ring_scatter(
        sems, nz, z, z_right, z_left, lambda i, o, j: part.at[o, y, i, :, ylo], nx, 1, bufs[8:12], drains
    )
    y2 = ring_scatter(
        sems, ny, y, y_right, y_left, lambda i, o, j: part.at[o, i, z, :, zhi], nx, 1, bufs[12:16], drains
    )
    merge((0.0, 2.0, joined(y1, z2)), (0.1, 1.0, joined(z1, y2)))

    r_base = sems.take(nx - 1)
    ends = [
        sems.copy(part.at[shifted(x, nx, k), y, z], xr.at[x], r_base + k - 1, x_peers[k - 1]) for k in range(1, nx)
    ]
    for copy in ends:
        copy.start()
    xr[x] = part[x, y, z]
    for k in range(1, nx):
        source = shifted(x, nx, nx - k)
        sems.copy(part.at[source, y, z], xr.at[source], r_base + k - 1, x_peers[k - 1]).wait_recv()
    for source in range(2):
        total = xr[source * hx]
        for k in range(1, hx):
            total = total + xr[source * hx + k]
        ig_out[source] = total.astype(BF16)

    for copy in ends:
        copy.wait_send()
    for drain in drains:
        drain()

    @pl.when(is_first)
    def _():
        for drain in first_drains:
            drain()
        dec0.wait_send()

    for copy in (dec1, enc1, pre1):
        copy.wait_send()
    fg_local.wait()
    fg_remote.wait_send()
    sems.copy(fg.at[c], fg_out.at[:, 1 - c], fg_index, sibling).wait_recv()


def scatter_buffers(n, outer, inner, columns):
    half = (2, outer, inner, HALF, columns)
    full = (max(n // 2 - 1, 1), 2, outer, inner, ROWS, columns)
    return [pltpu.VMEM(half, BF16)] * 2 + [pltpu.VMEM(full, BF16)] * 2


def body(nx, ny, cotangent, decoder, encoder, preact, block_ids, block_counts):
    nz = lax.axis_size("feat")
    num_layers = decoder.shape[1]
    feats, width = decoder.shape[0], cotangent.shape[2]
    windows = preact.shape[0] // WIN
    cut, rcut = width - 128, 256
    groups = nx * ny * 2 // num_layers
    local_blocks = feats // BLOCK
    layer = lax.axis_index("layer")
    source = layer // groups
    chip_layer = layer - layer % 2
    ids = lax.dynamic_index_in_dim(block_ids, source, 0, keepdims=False)
    counts = lax.dynamic_index_in_dim(block_counts, source, 0, keepdims=False)
    slot = (chip_layer % groups + jnp.arange(2)) * nz + lax.axis_index("feat")
    own = (slot[:, None] * local_blocks + jnp.arange(local_blocks)[None, :]).reshape(-1)
    live = jnp.arange(ids.shape[1])[None, :] < counts[:, None]
    found = jnp.any((ids[:, :, None] == own[None, None, :]) & live[:, :, None], axis=1)
    hit = jnp.broadcast_to(found[:, :, None], (windows, 2 * local_blocks, BLOCK)).reshape(windows, 1, 2 * feats)

    any_ref = pl.BlockSpec(memory_space=pl.ANY)
    vmem_ref = pl.BlockSpec(memory_space=pltpu.VMEM)
    tokens = nx * ny * ROWS
    pieces = (nx, ny, nz, ROWS, width)
    ycols = rcut + 128
    bufs = (
        scatter_buffers(ny, nx, nz, ycols)
        + scatter_buffers(nz, nx, ny, width - ycols)
        + scatter_buffers(nz, nx, 1, ycols)
        + scatter_buffers(ny, nx, 1, width - ycols)
    )
    count = 8 * (nx + ny + nz) * max(nx, ny)
    fg, ig = pl.pallas_call(
        functools.partial(kernel, (nx, ny, nz, cut, rcut, width)),
        out_shape=(
            jax.ShapeDtypeStruct((windows, 2, ROWS, feats), BF16),
            jax.ShapeDtypeStruct((num_layers, ROWS, width), BF16),
        ),
        in_specs=[any_ref] * 4 + [vmem_ref],
        out_specs=(any_ref, vmem_ref),
        scratch_shapes=[
            pltpu.VMEM(pieces, BF16),
            pltpu.VMEM(pieces, BF16),
            pltpu.VMEM((num_layers, 2, feats, nz * width), BF16),
            pltpu.VMEM((2, nz * width, feats), BF16),
            pltpu.VMEM((2, windows, ROWS, feats), BF16),
            pltpu.VMEM((2, windows, ROWS, feats), BF16),
            pltpu.VMEM((2, tokens, feats), F32),
            pltpu.VMEM(pieces, F32),
            pltpu.VMEM((nx, ROWS, width), F32),
            bufs,
            pltpu.SemaphoreType.DMA((count,)),
            pltpu.SemaphoreType.DMA((count,)),
            pltpu.SemaphoreType.DMA((7,)),
        ],
        compiler_params=pltpu.CompilerParams(
            collective_id=0, has_side_effects=True, vmem_limit_bytes=60 * 1024 * 1024
        ),
    )(
        cotangent,
        jnp.transpose(decoder, (1, 0, 2)),
        encoder,
        preact.reshape(windows, 2, ROWS, feats),
        hit.astype(F32),
    )
    return fg.reshape(windows * WIN, feats), ig


def solution(mesh, nx=4, ny=4):
    return jax.shard_map(
        functools.partial(body, nx, ny),
        mesh=mesh,
        in_specs=(
            P(None, "layer", "feat"),
            P(("layer", "feat"), None, None),
            P(None, ("layer", "feat")),
            P(None, ("layer", "feat")),
            P(),
            P(),
        ),
        out_specs=(P(None, ("layer", "feat")), P(None, "layer", "feat")),
        check_vma=False,
    )
```

time: 420 us -> 164 us (0.39)
  waiting for transfers between devices: 328 us -> 0 us
  Pallas kernels: 0 us -> 151 us
  blocking collectives: 31.7 us -> 0 us
  matrix products: 17.5 us -> 0 us
  between operations: 14.1 us -> 0.71 us
  starting transfers between devices: 7.54 us -> 0 us
    reduce_scatter x1 -> x0, waiting for transfers between devices: 220 us -> none  [body(): lax.psum_scatter(lax.dot_general(encoder, feature_grad, (((1,), (1,)), ((...]
    pallas_call x0 -> x1, Pallas kernels: none -> 151 us  [body(): pl.pallas_call(functools.partial(kernel, (nx, ny, nz, cut, rcut, width)),...]
    all_gather x1 -> x0, waiting for transfers between devices: 77.2 us -> none  [body(): piece = lax.all_gather(wide_rows, 'layer', axis=1, tiled=True)]
    all_gather x1 -> x0, blocking collectives: 31.7 us -> none  [body(): wide_rows = lax.all_gather(cotangent, 'feat', axis=2, tiled=True)]
    all_to_all x1 -> x0, waiting for transfers between devices: 30.5 us -> none  [body(): lax.all_to_all(partial_t, 'layer', split_axis=1, concat_axis=0, tiled=True)]
    dot_general x2 -> x0, matrix products: 17.5 us -> none  [the longest x1 8.85 us: add_target(): lax.dot_general(cot_rows, weights, (((1,), (1,)), ((), ())), preferred_el...]
    while x2 -> x0, local copies, waits for them, and re-layouts: 8.32 us -> none  [body(): lax.fori_loop(source, num_layers, add_target, jnp.zeros((piece.shape[1],...]
    all_to_all x1 -> x0, starting transfers between devices: 7.46 us -> none  [body(): lax.all_to_all(partial_t, 'layer', split_axis=1, concat_axis=0, tiled=True)]
  transfers between devices with their start and end apart: 3 -> 0, of which waited for: 3 -> 0; matrix products, arithmetic and copies ran while one was open for 3% -> 0% of each run, Pallas kernels for 0% -> 0%
where the time goes in v1:
time: 164 us; the launch traced here: 163 us
  Pallas kernels  151 us (92%)
  local copies, waits for them, and re-layouts  11 us (7%)
    pallas_call x1, Pallas kernels, body(): pl.pallas_call(functools.partial(kernel, (nx, ny, nz, cut, rcut, width)),...  151 us
    unnamed x5, local copies, waits for them, and re-layouts  9.48 us

profile of v1, /device:TPU:4, one launch (start us, length us, event | category | flops | bytes accessed | tf_op | source)
XLA Modules:
  0.0 163.1 jit_solution(14844770189116557673)
XLA Ops:
  0.6 0.0 copy-start
  0.7 0.7 dynamic-slice_bitcast_fusion.1
  1.4 0.1 iota_add_fusion
  1.5 0.1 add.64
  1.5 0.1 iota_compare_fusion
  1.6 0.0 copy-done
  1.6 0.2 and_reduce_fusion
  1.9 0.1 copy.10
  1.9 0.7 broadcast_in_dim.2
  2.6 6.1 %copy.12 = bf16[256,2,5120]{2,0,1:T(8,128)(2,1)} copy(bf16[256,2,5120]{2,1,0:T(2,128)(2,1)} %param.7) | data formatting | bytes 10485760 | tf_op args[1]
  8.7 151.0 %shard_map.77 = (bf16[16,2,32,256]{3,2,1,0:T(8,128)(2,1)}, bf16[2,32,640]{2,1,0:T(8,128)(2,1)}) custom-call(bf16[2,32,640]{2,1,0:T(8,128)(2,1)} %cot.1, bf16[2,256,5120]{2,1,0:T(8,128)(2,1)} %bitcast.10, bf16[5120,256]{1,0:T(8,128)(2,1)} %enc.1, bf16[16,2,32,256]{3,2,1,0:T(8,128)(2,1)} %bitcast.11, f32[16,1,512]{2,1,0:T(1,128)} %bitcast.13), custom_call_target="tpu_custom_call" | custom-call | tf_op jit(solution)/shard_map/pallas_call | solution.py:474
  159.7 1.9 %copy.15 = bf16[1024,256]{1,0:T(8,128)(2,1)} copy(bf16[1024,256]{1,0:T(8,128)(2,1)} %bitcast.12) | data formatting | bytes 1048576
  161.6 1.5 copy.16
  (3 shorter events, 0.0 us)
Async XLA Ops:
  0.6 1.0 copy-start

commit v2 on v1

--- a/solution.py
+++ b/solution.py
@@ -188,7 +188,43 @@
         stage()
 
 
-def kernel(dims, cot, dec, enc, pre, hit, fg_out, ig_out, g0, g1, dv, ev, pv, fg, acc, part, xr, bufs, send, recv, local):
+class Fan:
+    def __init__(self, sems, me, right, left, chunk, parts):
+        self.sems, self.me, self.sides, self.chunk, self.parts = sems, me, ((right, 3), (left, 1)), chunk, parts
+        self.base = sems.take(4 * parts)
+
+    def copies(self, step, number, part, sent):
+        found = []
+        for side, (device, by) in enumerate(self.sides):
+            at = lax.rem(self.me + by * (step - (1 if sent else 0)), 4)
+            ref = self.chunk(at, part, both(side) if step == 2 else pl.ds(0, ROWS))
+            index = self.base + (2 * (step - 1) + side) * self.parts + number
+            found.append(self.sems.copy(ref, ref, index, device))
+        return found
+
+    def first(self, number, part):
+        for copy in self.copies(1, number, part, True):
+            copy.start()
+
+    def second(self, number, part):
+        for copy in self.copies(1, number, part, False):
+            copy.wait_recv()
+        for copy in self.copies(2, number, part, True):
+            copy.start()
+
+    def arrived(self, number, part):
+        for copy in self.copies(2, number, part, False):
+            copy.wait_recv()
+
+    def sent(self, number, part):
+        for step in (1, 2):
+            for copy in self.copies(step, number, part, True):
+                copy.wait_send()
+
+
+def kernel(
+    dims, cot, dec, enc, pre, ids, counts, fg_out, ig_out, g0, g1, raw, dv, ev, pv, fg, hit, acc, part, xr, bufs, send, recv, local
+):
     nx, ny, nz, cut, rcut, width = dims
     hx = nx // 2
     layer = lax.axis_index("layer")
@@ -206,10 +242,11 @@
 
     sibling = device(x, y, z, 1 - c)
     x_peers = [device(shifted(x, nx, k), y, z, c) for k in range(1, nx)]
+    y_peers = [device(x, shifted(y, ny, k), z, c) for k in range(1, ny)]
     x_right, x_left = x_peers[0], x_peers[-1]
-    y_right, y_left = device(x, shifted(y, ny, 1), z, c), device(x, shifted(y, ny, ny - 1), z, c)
+    y_right, y_left = y_peers[0], y_peers[-1]
     z_right, z_left = device(x, y, shifted(z, nz, 1), c), device(x, y, shifted(z, nz, nz - 1), c)
-    peers = [sibling] + x_peers + [y_right, y_left, z_right, z_left]
+    peers = [sibling] + x_peers + y_peers + [z_right, z_left]
 
     own_copies = [
         pltpu.make_async_copy(cot.at[0], g0.at[x, y, z], local.at[0]),
@@ -221,12 +258,9 @@
     barrier = pltpu.get_barrier_semaphore()
     for peer in peers:
         pl.semaphore_signal(barrier, inc=1, device_id=peer, device_id_type=MESH)
-    weight_copies = [
-        pltpu.make_async_copy(dec.at[1], dv.at[1, c], local.at[2]),
-        pltpu.make_async_copy(dec.at[0], dv.at[0, c], local.at[3]),
-        pltpu.make_async_copy(enc, ev.at[c], local.at[4]),
-        pltpu.make_async_copy(pre.at[:, c], pv.at[c], local.at[5]),
-    ]
+    dec_local = pltpu.make_async_copy(dec, raw, local.at[2])
+    enc_local = pltpu.make_async_copy(enc, ev.at[c], local.at[3])
+    pre_local = pltpu.make_async_copy(pre.at[:, c], pv.at[c], local.at[4])
     for copy in own_copies:
         copy.wait()
     pl.semaphore_wait(barrier, len(peers))
@@ -234,107 +268,161 @@
     sems = Semaphores(send, recv)
     drains = []
 
+    def first_only(stage):
+        pl.when(is_first)(lambda: stage())
+
     lo, hi = pl.ds(0, cut), pl.ds(cut, width - cut)
     rlo, rhi = pl.ds(0, rcut), pl.ds(rcut, width - rcut)
-    a_base = sems.take(nx - 1)
-    t_base = sems.take(nx - 1)
-
-    def x_copy(k, sent, target):
-        at = x if sent else shifted(x, nx, nx - k)
-        if target:
-            ref = g1.at[at, y, z, :, hi]
-            return sems.copy(ref, ref, a_base + k - 1, x_peers[k - 1])
-        ref = g0.at[at, y, z]
-        return sems.copy(ref, ref, t_base + k - 1, x_peers[k - 1])
-
-    def x_start():
-        for k in range(1, nx):
-            x_copy(k, True, 1).start()
-            pl.when(shifted(x, nx, k) < hx)(lambda k=k: x_copy(k, True, 0).start())
-
-    def x_end():
-        for k in range(1, nx):
-            x_copy(k, False, 1).wait_recv()
-
-        @pl.when(is_first)
-        def _():
-            for k in range(1, nx):
-                x_copy(k, False, 0).wait_recv()
-
-    def x_drain():
-        for k in range(1, nx):
-            x_copy(k, True, 1).wait_send()
-            pl.when(shifted(x, nx, k) < hx)(lambda k=k: x_copy(k, True, 0).wait_send())
-
-    drains.append(x_drain)
-
-    az = ring_gather(sems, nz, z, z_right, z_left, lambda i, s, r: g1.at[x, y, i, r, lo], 1, drains)
-    ay = ring_gather(sems, ny, y, y_right, y_left, lambda i, s, r: g1.at[x, i, :, r, lo], 1, drains)
-    ax = ring_gather(sems, nx, x, x_right, x_left, lambda i, s, r: g1.at[i, s, :, r, lo], ny, drains)
-    bz = ring_gather(sems, nz, z, z_right, z_left, lambda i, s, r: g1.at[:, y, i, r, hi], 1, drains)
-    by = ring_gather(sems, ny, y, y_right, y_left, lambda i, s, r: g1.at[s, i, :, r, hi], nx, drains)
+
+    class Direct:
+        def __init__(self, n, me, to, chunk, wanted=None):
+            self.n, self.me, self.to, self.chunk, self.wanted = n, me, to, chunk, wanted
+            self.base = sems.take(n - 1)
+
+        def copy(self, k, sent):
+            ref = self.chunk(self.me if sent else shifted(self.me, self.n, self.n - k))
+            return sems.copy(ref, ref, self.base + k - 1, self.to[k - 1])
+
+        def each(self, act):
+            for k in range(1, self.n):
+                if self.wanted is None:
+                    act(k)
+                else:
+                    pl.when(self.wanted(shifted(self.me, self.n, k)))(lambda k=k: act(k))
+
+        def start(self):
+            self.each(lambda k: self.copy(k, True).start())
+
+        def arrived(self):
+            for k in range(1, self.n):
+                self.copy(k, False).wait_recv()
+
+        def sent(self):
+            self.each(lambda k: self.copy(k, True).wait_send())
+
+    ya = Direct(ny, y, y_peers, lambda i: g1.at[x, i, z, :, lo])
+    xt = Direct(nx, x, x_peers, lambda i: g0.at[i, y, z], lambda to: to < hx)
+    xb = Direct(nx, x, x_peers, lambda i: g1.at[i, y, z, :, hi])
+    yc = Direct(ny, y, y_peers, lambda i: g0.at[:, i, z, :, rhi])
     first_drains = []
-    dz = ring_gather(sems, nz, z, z_right, z_left, lambda i, s, r: g0.at[:, y, i, r, rlo], 1, first_drains)
-    dy = ring_gather(sems, ny, y, y_right, y_left, lambda i, s, r: g0.at[s, i, :, r, rlo], nx, first_drains)
-    cy = ring_gather(sems, ny, y, y_right, y_left, lambda i, s, r: g0.at[:, i, z, r, rhi], 1, first_drains)
-    cz = ring_gather(sems, nz, z, z_right, z_left, lambda i, s, r: g0.at[s, :, i, r, rhi], nx, first_drains)
-
-    def joined(*rings):
-        stages = list(rings[0])
-        for ring in rings[1:]:
-            end, start = stages.pop(), ring[0]
-
-            def link(end=end, start=start):
-                end()
-                start()
-
-            stages.append(link)
-            stages.extend(ring[1:])
-        return stages
-
-    def first_only(stages):
-        def wrap(stage):
-            return lambda: pl.when(is_first)(lambda: stage())
-
-        return [wrap(stage) for stage in stages]
-
-    dec1 = sems.copy(dec.at[1], dv.at[1, c], sems.take(), sibling)
-    dec0 = sems.copy(dec.at[0], dv.at[0, c], sems.take(), sibling)
+    za = ring_gather(sems, nz, z, z_right, z_left, lambda i, s, r: g1.at[x, :, i, r, lo], 1, drains)
+    zb = ring_gather(sems, nz, z, z_right, z_left, lambda i, s, r: g1.at[:, y, i, r, hi], 1, drains)
+    zd = ring_gather(sems, nz, z, z_right, z_left, lambda i, s, r: g0.at[:, y, i, r, rlo], 1, first_drains)
+    zc = ring_gather(sems, nz, z, z_right, z_left, lambda i, s, r: g0.at[s, :, i, r, rhi], nx, first_drains)
+    xa = Fan(sems, x, x_right, x_left, lambda i, p, r: g1.at[i, :, p, r, lo], nz)
+    yb = Fan(sems, y, y_right, y_left, lambda i, p, r: g1.at[:, i, p, r, hi], nz)
+    yd = Fan(sems, y, y_right, y_left, lambda i, p, r: g0.at[:, i, p, r, rlo], nz)
+
+    def each_part(step, act):
+        if step == 0:
+            act(0, z)
+        elif step == nz // 2:
+            act(nz - 1, shifted(z, nz, nz // 2))
+        else:
+            def loop(j, carry):
+                act(2 * step - 1 + j, lax.rem(z + nz + (2 * j - 1) * step, nz))
+                return carry
+
+            lax.fori_loop(0, 2, loop, 0)
+
+    feats = dv.shape[2]
+    dec1 = sems.copy(dv.at[1, c], dv.at[1, c], sems.take(), sibling)
+    dec0 = sems.copy(dv.at[0, c], dv.at[0, c], sems.take(), sibling)
     enc1 = sems.copy(enc, ev.at[c], sems.take(), sibling)
     pre1 = sems.copy(pre.at[:, 1 - c], pv.at[c], sems.take(), sibling)
 
-    def weights_start():
-        weight_copies[0].start()
-        dec1.start()
-
-        @pl.when(is_first)
-        def _():
-            weight_copies[1].start()
-            dec0.start()
-
-        for copy in weight_copies[2:] + [enc1, pre1]:
-            copy.start()
-
-    merge(
-        (0.0, 1.0, joined(az, ay, ax)),
-        (0.1, 1.0, [x_start]),
-        (0.2, 1.0, [weights_start]),
-        (0.9, 1.0, [x_end]),
-        (0.95, 1.0, joined(bz, by)),
-        (0.96, 1.0, first_only(joined(dz, dy))),
-        (0.97, 1.0, first_only(joined(cy, cz))),
-    )
+    def sort_targets(step):
+        def one(j, carry):
+            at = pl.multiple_of((step * 4 + j) * 16, 16)
+            dv[1, c, pl.ds(at, 16), :] = raw[pl.ds(at, 16)][:, 1, :]
+
+            @pl.when(is_first)
+            def _():
+                dv[0, c, pl.ds(at, 16), :] = raw[pl.ds(at, 16)][:, 0, :]
+
+            return carry
+
+        lax.fori_loop(0, 4, one, 0)
+
+    ya.start()
+    xb.start()
+    xt.start()
+    for copy in (dec_local, enc_local, pre_local, enc1, pre1):
+        copy.start()
+
+    ids_here = ids[layer // (nx * ny)]
+    counts_here = jnp.where(is_first, counts[0:1, :], counts[1:2, :]).astype(F32)
+    windows = nx * ny
+    square = (windows, windows)
+    diagonal = lax.broadcasted_iota(jnp.int32, square, 0) == lax.broadcasted_iota(jnp.int32, square, 1)
+    column = jnp.sum(jnp.where(diagonal, jnp.broadcast_to(counts_here, square), 0.0), axis=1, keepdims=True)
+    live_slots = lax.broadcasted_iota(jnp.int32, ids_here.shape, 1).astype(F32) < column
+    blocks = feats // BLOCK
+    for side in range(2):
+        slot = (lax.rem(layer - c, nx * ny) + side) * nz + z
+        for k in range(blocks):
+            same = (ids_here == slot * blocks + k) & live_slots
+            found = jnp.max(jnp.where(same, 1.0, 0.0), axis=1, keepdims=True)
+            hit[side * blocks + k] = jnp.broadcast_to(found, (windows, BLOCK))
+
+    ya.arrived()
+    za[0]()
+    xb.arrived()
+    first_only(xt.arrived)
+    zb[0]()
+    first_only(zd[0])
+    for step in range(nz // 2 + 1):
+        if step > 0:
+            za[step]()
+        each_part(step, xa.first)
+        if step > 0:
+            zb[step]()
+        each_part(step, yb.first)
+
+        def first_step(step=step):
+            if step > 0:
+                zd[step]()
+            each_part(step, yd.first)
+            if step == 0:
+                yc.start()
+            elif step == 1:
+                yc.arrived()
+            if step > 0:
+                zc[step - 1]()
+
+        first_only(first_step)
+        if step == 0:
+            dec_local.wait()
+        if step < nz // 2:
+            sort_targets(step)
+        if step == nz // 2 - 1:
+            dec1.start()
+            first_only(dec0.start)
+        if step > 0:
+            each_part(step - 1, xa.second)
+            each_part(step - 1, yb.second)
+            first_only(lambda step=step: each_part(step - 1, yd.second))
+    each_part(nz // 2, xa.second)
+    each_part(nz // 2, yb.second)
+
+    def first_last():
+        each_part(nz // 2, yd.second)
+        zc[nz // 2]()
+
+    first_only(first_last)
+
+    def numbered(act):
+        for step in range(nz // 2 + 1):
+            each_part(step, act)
+
+    numbered(xa.arrived)
+    numbered(yb.arrived)
+    first_only(lambda: numbered(yd.arrived))
 
     tokens = nx * ny * ROWS
-    feats = dv.shape[2]
     contract = (((1,), (1,)), ((), ()))
-    weight_copies[0].wait()
     dec1.wait_recv()
-
-    @pl.when(is_first)
-    def _():
-        weight_copies[1].wait()
-        dec0.wait_recv()
+    first_only(dec0.wait_recv)
 
     acc[...] = jnp.zeros_like(acc)
 
@@ -353,23 +441,25 @@
         return carry
 
     lax.fori_loop(0, nz, act_step, 0)
-    weight_copies[3].wait()
+    pre_local.wait()
     pre1.wait_recv()
 
     def mask_step(w, carry):
         for side in range(2):
-            live = (pv[side, w].astype(F32) > 0.0) & (hit[w, :, pl.ds(side * feats, feats)] > 0.0)
-            grad = jnp.where(live, acc[side, pl.ds(pl.multiple_of(w * ROWS, ROWS), ROWS), :], 0.0)
-            fg[side, w] = grad.astype(BF16)
+            for k in range(blocks):
+                lanes = pl.ds(k * BLOCK, BLOCK)
+                live = (pv[side, w, :, lanes].astype(F32) > 0.0) & (hit[side * blocks + k, pl.ds(w, 1), :] > 0.0)
+                grad = jnp.where(live, acc[side, pl.ds(pl.multiple_of(w * ROWS, ROWS), ROWS), lanes], 0.0)
+                fg[side, w, :, lanes] = grad.astype(BF16)
         return carry
 
     lax.fori_loop(0, nx * ny, mask_step, 0)
-    fg_local = pltpu.make_async_copy(fg.at[c], fg_out.at[:, c], local.at[6])
+    fg_local = pltpu.make_async_copy(fg.at[c], fg_out.at[:, c], local.at[5])
     fg_index = sems.take()
     fg_remote = sems.copy(fg.at[1 - c], fg_out.at[:, c], fg_index, sibling)
     fg_local.start()
     fg_remote.start()
-    weight_copies[2].wait()
+    enc_local.wait()
     enc1.wait_recv()
 
     def part_step(zz, carry):
@@ -385,7 +475,20 @@
 
     lax.fori_loop(0, nz, part_step, 0)
 
-    ylo, zhi = pl.ds(0, rcut + 128), pl.ds(rcut + 128, width - rcut - 128)
+    ylo, zhi = pl.ds(0, rcut), pl.ds(rcut, width - rcut)
+    def joined(*rings):
+        stages = list(rings[0])
+        for ring in rings[1:]:
+            end, start = stages.pop(), ring[0]
+
+            def link(end=end, start=start):
+                end()
+                start()
+
+            stages.append(link)
+            stages.extend(ring[1:])
+        return stages
+
     y1 = ring_scatter(
         sems, ny, y, y_right, y_left, lambda i, o, j: part.at[o, i, j, :, ylo], nx, nz, bufs[0:4], drains
     )
@@ -421,12 +524,19 @@
     for drain in drains:
         drain()
 
-    @pl.when(is_first)
-    def _():
+    for direct in (ya, xb, xt):
+        direct.sent()
+    numbered(xa.sent)
+    numbered(yb.sent)
+
+    def first_sent():
         for drain in first_drains:
             drain()
+        yc.sent()
+        numbered(yd.sent)
         dec0.wait_send()
 
+    first_only(first_sent)
     for copy in (dec1, enc1, pre1):
         copy.wait_send()
     fg_local.wait()
@@ -445,25 +555,12 @@
     num_layers = decoder.shape[1]
     feats, width = decoder.shape[0], cotangent.shape[2]
     windows = preact.shape[0] // WIN
-    cut, rcut = width - 128, 256
-    groups = nx * ny * 2 // num_layers
-    local_blocks = feats // BLOCK
-    layer = lax.axis_index("layer")
-    source = layer // groups
-    chip_layer = layer - layer % 2
-    ids = lax.dynamic_index_in_dim(block_ids, source, 0, keepdims=False)
-    counts = lax.dynamic_index_in_dim(block_counts, source, 0, keepdims=False)
-    slot = (chip_layer % groups + jnp.arange(2)) * nz + lax.axis_index("feat")
-    own = (slot[:, None] * local_blocks + jnp.arange(local_blocks)[None, :]).reshape(-1)
-    live = jnp.arange(ids.shape[1])[None, :] < counts[:, None]
-    found = jnp.any((ids[:, :, None] == own[None, None, :]) & live[:, :, None], axis=1)
-    hit = jnp.broadcast_to(found[:, :, None], (windows, 2 * local_blocks, BLOCK)).reshape(windows, 1, 2 * feats)
-
+    cut, rcut = width - 128, width - 256
     any_ref = pl.BlockSpec(memory_space=pl.ANY)
     vmem_ref = pl.BlockSpec(memory_space=pltpu.VMEM)
     tokens = nx * ny * ROWS
     pieces = (nx, ny, nz, ROWS, width)
-    ycols = rcut + 128
+    ycols = rcut
     bufs = (
         scatter_buffers(ny, nx, nz, ycols)
         + scatter_buffers(nz, nx, ny, width - ycols)
@@ -477,15 +574,17 @@
             jax.ShapeDtypeStruct((windows, 2, ROWS, feats), BF16),
             jax.ShapeDtypeStruct((num_layers, ROWS, width), BF16),
         ),
-        in_specs=[any_ref] * 4 + [vmem_ref],
+        in_specs=[any_ref] * 4 + [vmem_ref] * 2,
         out_specs=(any_ref, vmem_ref),
         scratch_shapes=[
             pltpu.VMEM(pieces, BF16),
             pltpu.VMEM(pieces, BF16),
+            pltpu.VMEM((feats, num_layers, nz * width), BF16),
             pltpu.VMEM((num_layers, 2, feats, nz * width), BF16),
             pltpu.VMEM((2, nz * width, feats), BF16),
             pltpu.VMEM((2, windows, ROWS, feats), BF16),
             pltpu.VMEM((2, windows, ROWS, feats), BF16),
+            pltpu.VMEM((2 * feats // BLOCK, windows, BLOCK), F32),
             pltpu.VMEM((2, tokens, feats), F32),
             pltpu.VMEM(pieces, F32),
             pltpu.VMEM((nx, ROWS, width), F32),
@@ -499,10 +598,11 @@
         ),
     )(
         cotangent,
-        jnp.transpose(decoder, (1, 0, 2)),
+        decoder,
         encoder,
         preact.reshape(windows, 2, ROWS, feats),
-        hit.astype(F32),
+        block_ids,
+        block_counts,
     )
     return fg.reshape(windows * WIN, feats), ig
 

time: 164 us -> 134 us (0.82)
  Pallas kernels: 151 us -> 129 us
  local copies, waits for them, and re-layouts: 11 us -> 3.4 us
    pallas_call x1, Pallas kernels: 151 us -> 129 us  [body(): pl.pallas_call(functools.partial(kernel, (nx, ny, nz, cut, rcut, width)),...]
    unnamed x5 -> x2, local copies, waits for them, and re-layouts: 9.48 us -> 3.4 us
where the time goes in v2:
time: 134 us; the launch traced here: 133 us
  Pallas kernels  129 us (96%)
  local copies, waits for them, and re-layouts  3.4 us (3%)
    pallas_call x1, Pallas kernels, body(): pl.pallas_call(functools.partial(kernel, (nx, ny, nz, cut, rcut, width)),...  129 us
    unnamed x2, local copies, waits for them, and re-layouts  3.4 us

profile of v2, /device:TPU:4, one launch (start us, length us, event | category | flops | bytes accessed | tf_op | source)
XLA Modules:
  0.0 133.3 jit_solution(9336076331482048267)
XLA Ops:
  0.6 129.2 %shard_map.77 = (bf16[16,2,32,256]{3,2,1,0:T(8,128)(2,1)}, bf16[2,32,640]{2,1,0:T(8,128)(2,1)}) custom-call(bf16[2,32,640]{2,1,0:T(8,128)(2,1)} %cot.1, bf16[256,2,5120]{2,1,0:T(2,128)(2,1)} %dec.1, bf16[5120,256]{1,0:T(8,128)(2,1)} %enc.1, bf16[16,2,32,256]{3,2,1,0:T(8,128)(2,1)} %bitcast.2, s32[2,16,32]{2,1,0:T(8,128)} %ids.1, s32[2,16]{1,0:T(2,128)} %counts.1), custom_call_target="tpu_custom_call" | custom-call | tf_op jit(solution)/shard_map/pallas_call | solution.py:571
  129.9 1.9 %copy.10 = bf16[1024,256]{1,0:T(8,128)(2,1)} copy(bf16[1024,256]{1,0:T(8,128)(2,1)} %bitcast.3) | data formatting | bytes 1048576
  131.8 1.5 %copy.11 = bf16[2,32,640]{2,1,0:T(8,128)(2,1)} copy(bf16[2,32,640]{2,1,0:T(8,128)(2,1)} %get-tuple-element.9) | data formatting | bytes 163840

commit v3 on v0

v3 whole, which is shorter than its diff:
```python
import functools

import jax
import jax.numpy as jnp
from jax import lax
from jax.experimental import pallas as pl
from jax.experimental.pallas import tpu as pltpu
from jax.sharding import PartitionSpec as P

MESH = pl.DeviceIdType.MESH
WIN = 64
ROWS = WIN // 2
WAVES = 2
STRIP = ROWS // WAVES
BLOCK = 128
SIDE = 4
F32 = jnp.float32
BF16 = jnp.bfloat16
WHOLE = pl.ds(0, SIDE)
CONTRACT = (((1,), (1,)), ((), ()))


def half(side):
    return pl.ds(side * (SIDE // 2), SIDE // 2)


def repeat(count, fn):
    if count == 1:
        fn(0)
        return

    def loop(i, carry):
        fn(i)
        return carry

    lax.fori_loop(0, count, loop, 0)


class Semaphores:
    def __init__(self, send, recv):
        self.send, self.recv, self.used = send, recv, 0

    def take(self, count=1):
        first = self.used
        self.used += count
        return first

    def copy(self, source, target, index, device):
        return pltpu.make_async_remote_copy(
            src_ref=source,
            dst_ref=target,
            send_sem=self.send.at[index],
            recv_sem=self.recv.at[index],
            device_id=device,
            device_id_type=MESH,
        )


class Direct:
    def __init__(self, sems, n, me, to, chunk, wanted=None):
        self.sems, self.n, self.me, self.to, self.chunk, self.wanted = sems, n, me, to, chunk, wanted
        self.base = sems.take(n - 1)

    def copy(self, k, sent):
        ref = self.chunk(self.me if sent else lax.rem(self.me + self.n - k, self.n))
        return self.sems.copy(ref, ref, self.base + k - 1, self.to[k - 1])

    def each(self, act):
        for k in range(1, self.n):
            if self.wanted is None:
                act(k)
            else:
                pl.when(self.wanted(lax.rem(self.me + k, self.n)))(lambda k=k: act(k))

    def start(self):
        self.each(lambda k: self.copy(k, True).start())

    def arrived(self):
        for k in range(1, self.n):
            self.copy(k, False).wait_recv()

    def sent(self):
        self.each(lambda k: self.copy(k, True).wait_send())


class Ring:
    def __init__(self, sems, n, me, right, left, chunk, parts):
        self.sems, self.n, self.me, self.sides = sems, n, me, ((right, -1), (left, 1))
        self.chunk, self.parts, self.steps = chunk, parts, n // 2
        self.base = sems.take(2 * self.steps * parts)

    def copies(self, step, number, part, sent):
        found = []
        for side, (device, sign) in enumerate(self.sides):
            at = lax.rem(self.me + self.n + sign * (step - (1 if sent else 0)), self.n)
            ref = self.chunk(at, part, half(side) if step == self.steps else WHOLE)
            index = self.base + (2 * (step - 1) + side) * self.parts + number
            found.append(self.sems.copy(ref, ref, index, device))
        return found

    def step(self, step, number=0, part=0):
        if step > 1:
            for copy in self.copies(step - 1, number, part, False):
                copy.wait_recv()
        if step <= self.steps:
            for copy in self.copies(step, number, part, True):
                copy.start()

    def sent(self, number=0, part=0):
        for step in range(1, self.steps + 1):
            for copy in self.copies(step, number, part, True):
                copy.wait_send()


class Scatter:
    def __init__(self, sems, n, me, right, left, own, outer, inner, columns, bufs):
        self.half_send, self.half_recv, self.full_send, self.full_recv = bufs
        self.sems, self.n, self.me, self.own, self.outer, self.inner = sems, n, me, own, outer, inner
        self.columns, self.steps = columns, n // 2
        self.sides = ((right, 1), (left, -1))
        self.base = sems.take(2 * self.steps * outer)

    def copy(self, step, side, o):
        index = self.base + ((step - 1) * 2 + side) * self.outer + o
        device = self.sides[side][0]
        if step == 1:
            return self.sems.copy(self.half_send.at[side, o], self.half_recv.at[side, o], index, device)
        return self.sems.copy(self.full_send.at[step - 2, side, o], self.full_recv.at[step - 2, side, o], index, device)

    def fill(self, step, side, o, at):
        own, count = self.own, self.inner // 2
        lanes = pl.ds(side * (self.columns // 2), self.columns // 2)
        others = pl.ds((1 - side) * (self.columns // 2), self.columns // 2)
        if step == 1 and self.inner == 1:
            self.half_send[side, o, 0] = own(at, o, 0)[:, lanes].astype(BF16)
        elif step == 1:
            def one(j):
                self.half_send[side, o, j] = own(at, o, side * count + j)[...].astype(BF16)

            repeat(count, one)
        elif step == 2 and self.inner == 1:
            ref = own(at, o, 0)
            self.full_send[0, side, o, 0, :, lanes] = (
                ref[:, lanes] + self.half_recv[side, o, 0].astype(F32)
            ).astype(BF16)
            self.full_send[0, side, o, 0, :, others] = ref[:, others].astype(BF16)
        elif step == 2:
            def one(j):
                mine, other = side * count + j, (1 - side) * count + j
                self.full_send[0, side, o, mine] = (
                    own(at, o, mine)[...] + self.half_recv[side, o, j].astype(F32)
                ).astype(BF16)
                self.full_send[0, side, o, other] = own(at, o, other)[...].astype(BF16)

            repeat(count, one)
        else:
            def one(j):
                self.full_send[step - 2, side, o, j] = (
                    own(at, o, j)[...] + self.full_recv[step - 3, side, o, j].astype(F32)
                ).astype(BF16)

            repeat(self.inner, one)

    def step(self, step, o):
        for side, (_, sign) in enumerate(self.sides):
            if step > 1:
                self.copy(step - 1, side, o).wait_recv()
            self.fill(step, side, o, lax.rem(self.me + self.n + sign * (self.steps - step + 1), self.n))
            self.copy(step, side, o).start()

    def final(self, o):
        for side in range(2):
            self.copy(self.steps, side, o).wait_recv()

        def add(j):
            ref = self.own(self.me, o, j)
            last = self.steps - 2
            ref[...] = ref[...] + self.full_recv[last, 0, o, j].astype(F32) + self.full_recv[last, 1, o, j].astype(F32)

        repeat(self.inner, add)

    def sent(self, o):
        for step in range(1, self.steps + 1):
            for side in range(2):
                self.copy(step, side, o).wait_send()


def kernel(
    dims, cot, dec, enc, pre, ids, counts, fg_out, ig_out, g0, g1, raw, dv, ev, pv, fg, hit, acc, part, xr, bufs, send, recv, local
):
    nx, ny, nz, rcut, ycut, width = dims
    hx = nx // 2
    windows, feats = nx * ny, dv.shape[2]
    layer = lax.axis_index("layer")
    z = lax.axis_index("feat")
    c = lax.rem(layer, 2)
    y = lax.rem(layer // 2, ny)
    x = layer // (2 * ny)
    is_first = x < hx

    def device(x, y, z, c):
        return ((x * ny + y) * 2 + c, z)

    def shifted(at, n, by):
        return lax.rem(at + by, n)

    def first_only(act):
        pl.when(is_first)(lambda: act())

    sibling = device(x, y, z, 1 - c)
    x_peers = [device(shifted(x, nx, k), y, z, c) for k in range(1, nx)]
    y_peers = [device(x, shifted(y, ny, k), z, c) for k in range(1, ny)]
    z_peers = [device(x, y, shifted(z, nz, k), c) for k in range(1, nz)]
    x_sides, y_sides, z_sides = [(to[0], to[-1]) for to in (x_peers, y_peers, z_peers)]
    peers = [sibling] + x_peers + y_peers + z_peers

    own_copies = [
        pltpu.make_async_copy(cot.at[0], g0.at[x, y, z], local.at[0]),
        pltpu.make_async_copy(cot.at[1], g1.at[x, y, z], local.at[1]),
    ]
    for copy in own_copies:
        copy.start()
    barrier = pltpu.get_barrier_semaphore()
    for peer in peers:
        pl.semaphore_signal(barrier, inc=1, device_id=peer, device_id_type=MESH)
    dec_local = pltpu.make_async_copy(dec, raw, local.at[2])
    enc_local = pltpu.make_async_copy(enc, ev.at[c], local.at[3])
    pre_local = pltpu.make_async_copy(pre.at[:, c], pv.at[c], local.at[4])
    for copy in own_copies:
        copy.wait()
    pl.semaphore_wait(barrier, len(peers))

    sems = Semaphores(send, recv)
    rlo, rhi = pl.ds(0, rcut), pl.ds(rcut, width - rcut)
    ylo, zhi = pl.ds(0, ycut), pl.ds(ycut, width - ycut)

    dec1 = sems.copy(dv.at[1, c], dv.at[1, c], sems.take(), sibling)
    dec0 = sems.copy(dv.at[0, c], dv.at[0, c], sems.take(), sibling)
    enc1 = sems.copy(enc, ev.at[c], sems.take(), sibling)
    pre1 = sems.copy(pre.at[:, 1 - c], pv.at[c], sems.take(), sibling)

    def sort_targets(quarter):
        def one(j):
            at = pl.multiple_of((quarter * (feats // 64) + j) * 16, 16)
            dv[1, c, pl.ds(at, 16), :] = raw[pl.ds(at, 16)][:, 1, :]

            @pl.when(is_first)
            def _():
                dv[0, c, pl.ds(at, 16), :] = raw[pl.ds(at, 16)][:, 0, :]

        repeat(feats // 64, one)

    def each_part(step, act):
        if step == 0:
            act(0, z)
        elif step == nz // 2:
            act(nz - 1, shifted(z, nz, nz // 2))
        else:
            repeat(2, lambda j: act(2 * step - 1 + j, lax.rem(z + nz + (2 * j - 1) * step, nz)))

    def all_parts(act):
        for step in range(nz // 2 + 1):
            each_part(step, act)

    def find_blocks():
        ids_here = ids[layer // windows]
        counts_here = jnp.where(is_first, counts[0:1, :], counts[1:2, :]).astype(F32)
        square = (windows, windows)
        diagonal = lax.broadcasted_iota(jnp.int32, square, 0) == lax.broadcasted_iota(jnp.int32, square, 1)
        column = jnp.sum(jnp.where(diagonal, jnp.broadcast_to(counts_here, square), 0.0), axis=1, keepdims=True)
        live_slots = lax.broadcasted_iota(jnp.int32, ids_here.shape, 1).astype(F32) < column
        for side in range(2):
            slot = (lax.rem(layer - c, windows) + side) * nz + z
            for k in range(feats // BLOCK):
                same = (ids_here == slot * (feats // BLOCK) + k) & live_slots
                found = jnp.max(jnp.where(same, 1.0, 0.0), axis=1, keepdims=True)
                hit[side * (feats // BLOCK) + k] = jnp.broadcast_to(found, (windows, BLOCK))

    class Wave:
        def __init__(self, wave):
            rows = pl.ds(wave * STRIP, STRIP)
            self.wave, self.rows = wave, rows
            self.ya = Direct(sems, ny, y, y_peers, lambda i: g1.at[x, i, z, rows, :])
            self.xt = Direct(sems, nx, x, x_peers, lambda i: g0.at[i, y, z, rows, :], lambda to: to < hx)
            self.yc = Direct(sems, ny, y, y_peers, lambda i: g0.at[:, i, z, rows, rhi])
            self.za = Ring(sems, nz, z, *z_sides, lambda i, p, h: g1.at[x, h, i, rows, :], 1)
            self.zd = Ring(sems, nz, z, *z_sides, lambda i, p, h: g0.at[h, y, i, rows, rlo], 1)
            self.zc = Ring(sems, nz, z, *z_sides, lambda i, p, h: g0.at[p, h, i, rows, rhi], nx)
            self.xa = Ring(sems, nx, x, *x_sides, lambda i, p, h: g1.at[i, h, p, rows, :], nz)
            self.yd = Ring(sems, ny, y, *y_sides, lambda i, p, h: g0.at[h, i, p, rows, rlo], nz)
            own = bufs[wave]
            self.y1 = Scatter(
                sems, ny, y, *y_sides, lambda i, o, j: part.at[o, i, j, rows, ylo], nx, nz, ycut, own[0:4]
            )
            self.z1 = Scatter(
                sems, nz, z, *z_sides, lambda i, o, j: part.at[o, j, i, rows, zhi], nx, ny, width - ycut, own[4:8]
            )
            self.y2 = Scatter(
                sems, ny, y, *y_sides, lambda i, o, j: part.at[o, i, z, rows, zhi], nx, 1, width - ycut, own[8:12]
            )
            self.z_send, self.z_recv = own[12:14]
            self.z2_base = sems.take(nx * nz)
            self.end_base = sems.take(nx)
            self.fg_base = sems.take()

        def begin(self):
            self.ya.start()
            self.xt.start()

        def gather(self, step):
            if step == 0:
                self.ya.arrived()
            self.za.step(step + 1)
            each_part(step, lambda n, p: self.xa.step(1, n, p))

            def first():
                if step == 0:
                    self.xt.arrived()
                self.zd.step(step + 1)
                each_part(step, lambda n, p: self.yd.step(1, n, p))
                if step == 0:
                    self.yc.start()
                elif step == 1:
                    self.yc.arrived()
                if step > 0:
                    repeat(nx, lambda s: self.zc.step(step, s, s))

            first_only(first)
            if step > 0:
                each_part(step - 1, lambda n, p: self.xa.step(2, n, p))
                first_only(lambda: each_part(step - 1, lambda n, p: self.yd.step(2, n, p)))

        def gather_last(self):
            each_part(nz // 2, lambda n, p: self.xa.step(2, n, p))

            def first():
                each_part(nz // 2, lambda n, p: self.yd.step(2, n, p))
                repeat(nx, lambda s: self.zc.step(nz // 2 + 1, s, s))

            first_only(first)

        def gathered(self):
            all_parts(lambda n, p: self.xa.step(3, n, p))
            first_only(lambda: all_parts(lambda n, p: self.yd.step(3, n, p)))

        def act(self):
            tokens = windows * STRIP

            def one(zz):
                columns = pl.ds(pl.multiple_of(zz * width, 128), width)
                rows1 = g1[:, :, zz, self.rows, :].reshape(tokens, width)
                for side in range(2):
                    term = lax.dot_general(rows1, dv[1, side, :, columns], CONTRACT, preferred_element_type=F32)
                    acc[side] += term

                @pl.when(is_first)
                def _():
                    rows0 = g0[:, :, zz, self.rows, :].reshape(tokens, width)
                    for side in range(2):
                        term = lax.dot_general(rows0, dv[0, side, :, columns], CONTRACT, preferred_element_type=F32)
                        acc[side] += term

            acc[...] = jnp.zeros_like(acc)
            repeat(nz, one)

        def mask(self):
            def one(w):
                at = pl.ds(pl.multiple_of(w * STRIP, STRIP), STRIP)
                for side in range(2):
                    for k in range(feats // BLOCK):
                        lanes = pl.ds(k * BLOCK, BLOCK)
                        found = hit[side * (feats // BLOCK) + k, pl.ds(w, 1), :] > 0.0
                        live = (pv[side, w, self.rows, lanes].astype(F32) > 0.0) & found
                        fg[side, w, self.rows, lanes] = jnp.where(live, acc[side, at, lanes], 0.0).astype(BF16)

            repeat(windows, one)
            self.fg_copy("local").start()
            self.fg_copy("sent").start()

        def fg_copy(self, which):
            rows = self.rows
            if which == "local":
                return pltpu.make_async_copy(fg.at[c, :, rows], fg_out.at[:, c, rows], local.at[5 + self.wave])
            to = c if which == "sent" else 1 - c
            return sems.copy(fg.at[1 - c, :, rows], fg_out.at[:, to, rows], self.fg_base, sibling)

        def partial(self):
            def one(zz):
                at = pl.ds(pl.multiple_of(zz * width, 128), width)
                total = None
                for side in range(2):
                    grads = fg[side, :, self.rows, :].reshape(windows * STRIP, feats)
                    term = lax.dot_general(grads, ev[side, at, :], CONTRACT, preferred_element_type=F32)
                    total = term if total is None else total + term
                part[:, :, zz, self.rows, :] = total.reshape(nx, ny, STRIP, width)

            repeat(nz, one)

        def z2_copy(self, o, k, sent):
            at = lax.rem(z + k, nz) if sent else lax.rem(z + nz - k, nz)
            index = self.z2_base + o * nz + k
            to = (layer, lax.rem(z + k, nz))
            if sent:
                return sems.copy(self.z_send.at[o, at], self.z_recv.at[o, z], index, to)
            return sems.copy(self.z_send.at[o, at], self.z_recv.at[o, at], index, to)

        def z2_start(self, o):
            def one(k):
                at = lax.rem(z + k + 1, nz)
                self.z_send[o, at] = part[o, y, at, self.rows, ylo].astype(BF16)
                self.z2_copy(o, k + 1, True).start()

            repeat(nz - 1, one)

        def z2_final(self, o):
            total = part[o, y, z, self.rows, ylo]
            for k in range(1, nz):
                self.z2_copy(o, k, False).wait_recv()
            for k in range(1, nz):
                total = total + self.z_recv[o, lax.rem(z + nz - k, nz)].astype(F32)
            part[o, y, z, self.rows, ylo] = total

        def reduce(self, stage):
            steps = nz // 2
            if stage == 1:
                repeat(nx, lambda o: self.y1.step(1, o))
                repeat(nx, lambda o: self.z1.step(1, o))
            elif stage == 2:
                repeat(nx, lambda o: self.y1.step(2, o))
                repeat(nx, lambda o: self.z1.step(2, o))
            elif stage == 3:
                repeat(nx, lambda o: self.z1.step(3, o))
            elif stage == 4:
                def one(o):
                    self.y1.final(o)
                    self.z2_start(o)

                repeat(nx, one)
            elif stage == 5:
                repeat(nx, lambda o: self.z1.step(4, o))
            elif stage == 6:
                def one(o):
                    self.z1.final(o)
                    self.y2.step(1, o)

                repeat(nx, one)
            elif stage == 7:
                repeat(nx, lambda o: self.y2.step(2, o))
                repeat(nx, self.z2_final)
            elif stage == 8:
                repeat(nx, self.y2.final)
                for k in range(1, nx):
                    self.end_copy(k, True).start()
                xr[x, self.rows] = part[x, y, z, self.rows, :]

        def end_copy(self, k, sent):
            if sent:
                to = shifted(x, nx, k)
                source, target = part.at[to, y, z, self.rows], xr.at[x, self.rows]
            else:
                at = shifted(x, nx, nx - k)
                source, target = part.at[at, y, z, self.rows], xr.at[at, self.rows]
            return sems.copy(source, target, self.end_base + k, x_peers[k - 1])

        def finish(self):
            for k in range(1, nx):
                self.end_copy(k, False).wait_recv()
            for source in range(2):
                total = xr[source * hx, self.rows]
                for k in range(1, hx):
                    total = total + xr[source * hx + k, self.rows]
                ig_out[source, self.rows] = total.astype(BF16)

        def drain(self):
            self.ya.sent()
            self.xt.sent()
            self.za.sent()
            all_parts(self.xa.sent)

            def first():
                self.yc.sent()
                self.zd.sent()
                repeat(nx, lambda s: self.zc.sent(s, s))
                all_parts(self.yd.sent)

            first_only(first)

            def one(o):
                self.y1.sent(o)
                self.z1.sent(o)
                self.y2.sent(o)
                repeat(nz - 1, lambda k: self.z2_copy(o, k + 1, True).wait_send())

            repeat(nx, one)
            for k in range(1, nx):
                self.end_copy(k, True).wait_send()
            self.fg_copy("local").wait()
            self.fg_copy("sent").wait_send()
            self.fg_copy("arrived").wait_recv()

    one, two = Wave(0), Wave(1)
    one.begin()
    for copy in (dec_local, enc_local, pre_local, enc1, pre1):
        copy.start()
    find_blocks()
    one.gather(0)
    dec_local.wait()
    sort_targets(0)
    one.gather(1)
    sort_targets(1)
    one.gather(2)
    two.begin()
    sort_targets(2)
    one.gather(3)
    two.gather(0)
    sort_targets(3)
    dec1.start()
    first_only(dec0.start)
    one.gather(4)
    two.gather(1)
    one.gather_last()
    two.gather(2)
    dec1.wait_recv()
    first_only(dec0.wait_recv)
    pre_local.wait()
    pre1.wait_recv()
    enc_local.wait()
    enc1.wait_recv()
    one.gathered()
    one.act()
    two.gather(3)
    one.mask()
    one.partial()
    one.reduce(1)
    two.gather(4)
    one.reduce(2)
    two.gather_last()
    one.reduce(3)
    one.reduce(4)
    one.reduce(5)
    two.gathered()
    two.act()
    two.mask()
    one.reduce(6)
    two.partial()
    two.reduce(1)
    one.reduce(7)
    two.reduce(2)
    one.reduce(8)
    two.reduce(3)
    two.reduce(4)
    two.reduce(5)
    one.finish()
    two.reduce(6)
    two.reduce(7)
    two.reduce(8)
    one.drain()
    two.finish()
    two.drain()
    for copy in (dec1, enc1, pre1):
        copy.wait_send()
    first_only(dec0.wait_send)


def scatter_buffers(n, outer, inner, columns):
    few = (2, outer, inner // 2, STRIP, columns) if inner > 1 else (2, outer, 1, STRIP, columns // 2)
    full = (n // 2 - 1, 2, outer, inner, STRIP, columns)
    return [pltpu.VMEM(few, BF16)] * 2 + [pltpu.VMEM(full, BF16)] * 2


def body(cotangent, decoder, encoder, preact, block_ids, block_counts):
    nx = ny = SIDE
    nz = lax.axis_size("feat")
    num_layers = decoder.shape[1]
    feats, width = decoder.shape[0], cotangent.shape[2]
    windows = preact.shape[0] // WIN
    rcut, ycut = width - 128, width - 256
    any_ref = pl.BlockSpec(memory_space=pl.ANY)
    vmem_ref = pl.BlockSpec(memory_space=pltpu.VMEM)
    pieces = (nx, ny, nz, ROWS, width)
    bufs = [
        scatter_buffers(ny, nx, nz, ycut)
        + scatter_buffers(nz, nx, ny, width - ycut)
        + scatter_buffers(ny, nx, 1, width - ycut)
        + [pltpu.VMEM((nx, nz, STRIP, ycut), BF16)] * 2
    ] * WAVES
    fg, ig = pl.pallas_call(
        functools.partial(kernel, (nx, ny, nz, rcut, ycut, width)),
        out_shape=(
            jax.ShapeDtypeStruct((windows, 2, ROWS, feats), BF16),
            jax.ShapeDtypeStruct((num_layers, ROWS, width), BF16),
        ),
        in_specs=[any_ref] * 4 + [vmem_ref] * 2,
        out_specs=(any_ref, vmem_ref),
        scratch_shapes=[
            pltpu.VMEM(pieces, BF16),
            pltpu.VMEM(pieces, BF16),
            pltpu.VMEM((feats, num_layers, nz * width), BF16),
            pltpu.VMEM((num_layers, 2, feats, nz * width), BF16),
            pltpu.VMEM((2, nz * width, feats), BF16),
            pltpu.VMEM((2, windows, ROWS, feats), BF16),
            pltpu.VMEM((2, windows, ROWS, feats), BF16),
            pltpu.VMEM((2 * feats // BLOCK, windows, BLOCK), F32),
            pltpu.VMEM((2, windows * STRIP, feats), F32),
            pltpu.VMEM(pieces, F32),
            pltpu.VMEM((nx, ROWS, width), F32),
            bufs,
            pltpu.SemaphoreType.DMA((512,)),
            pltpu.SemaphoreType.DMA((512,)),
            pltpu.SemaphoreType.DMA((5 + WAVES,)),
        ],
        compiler_params=pltpu.CompilerParams(
            collective_id=0, has_side_effects=True, vmem_limit_bytes=60 * 1024 * 1024
        ),
    )(cotangent, decoder, encoder, preact.reshape(windows, 2, ROWS, feats), block_ids, block_counts)
    return fg.reshape(windows * WIN, feats), ig


def solution(mesh):
    return jax.shard_map(
        body,
        mesh=mesh,
        in_specs=(
            P(None, "layer", "feat"),
            P(("layer", "feat"), None, None),
            P(None, ("layer", "feat")),
            P(None, ("layer", "feat")),
            P(),
            P(),
        ),
        out_specs=(P(None, ("layer", "feat")), P(None, "layer", "feat")),
        check_vma=False,
    )
```

time: 420 us -> 134 us (0.32)
  waiting for transfers between devices: 328 us -> 0 us
  Pallas kernels: 0 us -> 129 us
  blocking collectives: 31.7 us -> 0 us
  matrix products: 17.5 us -> 0 us
  between operations: 14.1 us -> 0.64 us
  local copies, waits for them, and re-layouts: 13.4 us -> 3.4 us
  starting transfers between devices: 7.54 us -> 0 us
  other arithmetic: 4.28 us -> 0 us
    reduce_scatter x1 -> x0, waiting for transfers between devices: 220 us -> none  [body(): lax.psum_scatter(lax.dot_general(encoder, feature_grad, (((1,), (1,)), ((...]
    pallas_call x0 -> x1, Pallas kernels: none -> 129 us  [body(): pl.pallas_call(functools.partial(kernel, (nx, ny, nz, rcut, ycut, width))...]
    all_gather x1 -> x0, waiting for transfers between devices: 77.2 us -> none  [body(): piece = lax.all_gather(wide_rows, 'layer', axis=1, tiled=True)]
    all_gather x1 -> x0, blocking collectives: 31.7 us -> none  [body(): wide_rows = lax.all_gather(cotangent, 'feat', axis=2, tiled=True)]
    all_to_all x1 -> x0, waiting for transfers between devices: 30.5 us -> none  [body(): lax.all_to_all(partial_t, 'layer', split_axis=1, concat_axis=0, tiled=True)]
    dot_general x2 -> x0, matrix products: 17.5 us -> none  [the longest x1 8.85 us: add_target(): lax.dot_general(cot_rows, weights, (((1,), (1,)), ((), ())), preferred_el...]
    while x2 -> x0, local copies, waits for them, and re-layouts: 8.32 us -> none  [body(): lax.fori_loop(source, num_layers, add_target, jnp.zeros((piece.shape[1],...]
    all_to_all x1 -> x0, starting transfers between devices: 7.46 us -> none  [body(): lax.all_to_all(partial_t, 'layer', split_axis=1, concat_axis=0, tiled=True)]
  transfers between devices with their start and end apart: 3 -> 0, of which waited for: 3 -> 0; matrix products, arithmetic and copies ran while one was open for 3% -> 0% of each run, Pallas kernels for 0% -> 0%
where the time goes in v3:
time: 134 us; the launch traced here: 133 us
  Pallas kernels  129 us (96%)
  local copies, waits for them, and re-layouts  3.4 us (3%)
    pallas_call x1, Pallas kernels, body(): pl.pallas_call(functools.partial(kernel, (nx, ny, nz, rcut, ycut, width))...  129 us
    unnamed x2, local copies, waits for them, and re-layouts  3.4 us

profile of v3, /device:TPU:4, one launch (start us, length us, event | category | flops | bytes accessed | tf_op | source)
XLA Modules:
  0.0 133.0 jit_solution(13113143955863716595)
XLA Ops:
  0.6 129.0 %shard_map.77 = (bf16[16,2,32,256]{3,2,1,0:T(8,128)(2,1)}, bf16[2,32,640]{2,1,0:T(8,128)(2,1)}) custom-call(bf16[2,32,640]{2,1,0:T(8,128)(2,1)} %cot.1, bf16[256,2,5120]{2,1,0:T(2,128)(2,1)} %dec.1, bf16[5120,256]{1,0:T(8,128)(2,1)} %enc.1, bf16[16,2,32,256]{3,2,1,0:T(8,128)(2,1)} %bitcast.2, s32[2,16,32]{2,1,0:T(8,128)} %ids.1, s32[2,16]{1,0:T(2,128)} %counts.1), custom_call_target="tpu_custom_call" | custom-call | tf_op jit(solution)/shard_map/pallas_call | solution.py:587
  129.6 1.9 %copy.10 = bf16[1024,256]{1,0:T(8,128)(2,1)} copy(bf16[1024,256]{1,0:T(8,128)(2,1)} %bitcast.3) | data formatting | bytes 1048576
  131.5 1.5 %copy.11 = bf16[2,32,640]{2,1,0:T(8,128)(2,1)} copy(bf16[2,32,640]{2,1,0:T(8,128)(2,1)} %get-tuple-element.9) | data formatting | bytes 163840

commit v4 on v3

--- a/solution.py
+++ b/solution.py
@@ -113,10 +113,10 @@
 
 
 class Scatter:
-    def __init__(self, sems, n, me, right, left, own, outer, inner, columns, bufs):
+    def __init__(self, sems, n, me, right, left, own, outer, inner, bufs):
         self.half_send, self.half_recv, self.full_send, self.full_recv = bufs
         self.sems, self.n, self.me, self.own, self.outer, self.inner = sems, n, me, own, outer, inner
-        self.columns, self.steps = columns, n // 2
+        self.steps = n // 2
         self.sides = ((right, 1), (left, -1))
         self.base = sems.take(2 * self.steps * outer)
 
@@ -128,38 +128,19 @@
         return self.sems.copy(self.full_send.at[step - 2, side, o], self.full_recv.at[step - 2, side, o], index, device)
 
     def fill(self, step, side, o, at):
-        own, count = self.own, self.inner // 2
-        lanes = pl.ds(side * (self.columns // 2), self.columns // 2)
-        others = pl.ds((1 - side) * (self.columns // 2), self.columns // 2)
-        if step == 1 and self.inner == 1:
-            self.half_send[side, o, 0] = own(at, o, 0)[:, lanes].astype(BF16)
-        elif step == 1:
-            def one(j):
-                self.half_send[side, o, j] = own(at, o, side * count + j)[...].astype(BF16)
-
-            repeat(count, one)
-        elif step == 2 and self.inner == 1:
-            ref = own(at, o, 0)
-            self.full_send[0, side, o, 0, :, lanes] = (
-                ref[:, lanes] + self.half_recv[side, o, 0].astype(F32)
+        count = self.inner // 2
+        mine, others = pl.ds(side * count, count), pl.ds((1 - side) * count, count)
+        if step == 1:
+            self.half_send[side, o] = self.own(at, o, mine)[...].astype(BF16)
+        elif step == 2:
+            self.full_send[0, side, o, mine] = (
+                self.own(at, o, mine)[...] + self.half_recv[side, o].astype(F32)
             ).astype(BF16)
-            self.full_send[0, side, o, 0, :, others] = ref[:, others].astype(BF16)
-        elif step == 2:
-            def one(j):
-                mine, other = side * count + j, (1 - side) * count + j
-                self.full_send[0, side, o, mine] = (
-                    own(at, o, mine)[...] + self.half_recv[side, o, j].astype(F32)
-                ).astype(BF16)
-                self.full_send[0, side, o, other] = own(at, o, other)[...].astype(BF16)
-
-            repeat(count, one)
+            self.full_send[0, side, o, others] = self.own(at, o, others)[...].astype(BF16)
         else:
-            def one(j):
-                self.full_send[step - 2, side, o, j] = (
-                    own(at, o, j)[...] + self.full_recv[step - 3, side, o, j].astype(F32)
-                ).astype(BF16)
-
-            repeat(self.inner, one)
+            self.full_send[step - 2, side, o] = (
+                self.own(at, o, pl.ds(0, self.inner))[...] + self.full_recv[step - 3, side, o].astype(F32)
+            ).astype(BF16)
 
     def step(self, step, o):
         for side, (_, sign) in enumerate(self.sides):
@@ -171,18 +152,41 @@
     def final(self, o):
         for side in range(2):
             self.copy(self.steps, side, o).wait_recv()
-
-        def add(j):
-            ref = self.own(self.me, o, j)
-            last = self.steps - 2
-            ref[...] = ref[...] + self.full_recv[last, 0, o, j].astype(F32) + self.full_recv[last, 1, o, j].astype(F32)
-
-        repeat(self.inner, add)
+        ref = self.own(self.me, o, pl.ds(0, self.inner))
+        last = self.steps - 2
+        ref[...] = ref[...] + self.full_recv[last, 0, o].astype(F32) + self.full_recv[last, 1, o].astype(F32)
 
     def sent(self, o):
         for step in range(1, self.steps + 1):
             for side in range(2):
                 self.copy(step, side, o).wait_send()
+
+
+class Exchange:
+    def __init__(self, sems, n, me, to, own, outer, bufs):
+        self.sems, self.n, self.me, self.to, self.own = sems, n, me, to, own
+        self.send, self.recv = bufs
+        self.base = sems.take(n * outer)
+
+    def copy(self, o, k, sent):
+        at = lax.rem(self.me + (k if sent else self.n - k), self.n)
+        target = self.me if sent else at
+        return self.sems.copy(self.send.at[o, at], self.recv.at[o, target], self.base + o * self.n + k, self.to(k))
+
+    def start(self, o):
+        self.send[o] = self.own(o, pl.ds(0, self.n))[...].astype(BF16)
+        repeat(self.n - 1, lambda k: self.copy(o, k + 1, True).start())
+
+    def final(self, o):
+        total = self.own(o, self.me)[...]
+        for k in range(1, self.n):
+            self.copy(o, k, False).wait_recv()
+        for k in range(1, self.n):
+            total = total + self.recv[o, lax.rem(self.me + self.n - k, self.n)].astype(F32)
+        self.own(o, self.me)[...] = total
+
+    def sent(self, o):
+        repeat(self.n - 1, lambda k: self.copy(o, k + 1, True).wait_send())
 
 
 def kernel(
@@ -290,16 +294,18 @@
             self.yd = Ring(sems, ny, y, *y_sides, lambda i, p, h: g0.at[h, i, p, rows, rlo], nz)
             own = bufs[wave]
             self.y1 = Scatter(
-                sems, ny, y, *y_sides, lambda i, o, j: part.at[o, i, j, rows, ylo], nx, nz, ycut, own[0:4]
+                sems, ny, y, *y_sides, lambda i, o, js: part.at[o, i, js, rows, ylo], nx, nz, own[0:4]
             )
             self.z1 = Scatter(
-                sems, nz, z, *z_sides, lambda i, o, j: part.at[o, j, i, rows, zhi], nx, ny, width - ycut, own[4:8]
+                sems, nz, z, *z_sides, lambda i, o, js: part.at[o, js, i, rows, zhi], nx, ny, own[4:8]
             )
-            self.y2 = Scatter(
-                sems, ny, y, *y_sides, lambda i, o, j: part.at[o, i, z, rows, zhi], nx, 1, width - ycut, own[8:12]
+            self.z2 = Exchange(
+                sems, nz, z, lambda k: (layer, shifted(z, nz, k)), lambda o, i: part.at[o, y, i, rows, ylo], nx, own[8:10]
             )
-            self.z_send, self.z_recv = own[12:14]
-            self.z2_base = sems.take(nx * nz)
+            self.y2 = Exchange(
+                sems, ny, y, lambda k: device(x, shifted(y, ny, k), z, c),
+                lambda o, i: part.at[o, i, z, rows, zhi], nx, own[10:12],
+            )
             self.end_base = sems.take(nx)
             self.fg_base = sems.take()
 
@@ -396,75 +402,40 @@
 
             repeat(nz, one)
 
-        def z2_copy(self, o, k, sent):
-            at = lax.rem(z + k, nz) if sent else lax.rem(z + nz - k, nz)
-            index = self.z2_base + o * nz + k
-            to = (layer, lax.rem(z + k, nz))
-            if sent:
-                return sems.copy(self.z_send.at[o, at], self.z_recv.at[o, z], index, to)
-            return sems.copy(self.z_send.at[o, at], self.z_recv.at[o, at], index, to)
-
-        def z2_start(self, o):
-            def one(k):
-                at = lax.rem(z + k + 1, nz)
-                self.z_send[o, at] = part[o, y, at, self.rows, ylo].astype(BF16)
-                self.z2_copy(o, k + 1, True).start()
-
-            repeat(nz - 1, one)
-
-        def z2_final(self, o):
-            total = part[o, y, z, self.rows, ylo]
-            for k in range(1, nz):
-                self.z2_copy(o, k, False).wait_recv()
-            for k in range(1, nz):
-                total = total + self.z_recv[o, lax.rem(z + nz - k, nz)].astype(F32)
-            part[o, y, z, self.rows, ylo] = total
-
         def reduce(self, stage):
-            steps = nz // 2
-            if stage == 1:
-                repeat(nx, lambda o: self.y1.step(1, o))
-                repeat(nx, lambda o: self.z1.step(1, o))
-            elif stage == 2:
-                repeat(nx, lambda o: self.y1.step(2, o))
-                repeat(nx, lambda o: self.z1.step(2, o))
-            elif stage == 3:
-                repeat(nx, lambda o: self.z1.step(3, o))
-            elif stage == 4:
+            if stage <= nz // 2:
+                repeat(nx, lambda o: self.z1.step(stage, o))
+                if stage <= ny // 2:
+                    repeat(nx, lambda o: self.y1.step(stage, o))
+            elif stage == 5:
                 def one(o):
                     self.y1.final(o)
-                    self.z2_start(o)
+                    self.z2.start(o)
 
                 repeat(nx, one)
-            elif stage == 5:
-                repeat(nx, lambda o: self.z1.step(4, o))
             elif stage == 6:
                 def one(o):
                     self.z1.final(o)
-                    self.y2.step(1, o)
+                    self.y2.start(o)
 
                 repeat(nx, one)
-            elif stage == 7:
-                repeat(nx, lambda o: self.y2.step(2, o))
-                repeat(nx, self.z2_final)
-            elif stage == 8:
-                repeat(nx, self.y2.final)
-                for k in range(1, nx):
-                    self.end_copy(k, True).start()
+            else:
+                def one(o):
+                    self.z2.final(o)
+                    self.y2.final(o)
+                    pl.when(o != x)(lambda: self.end_copy(o, True).start())
+
+                repeat(nx, one)
                 xr[x, self.rows] = part[x, y, z, self.rows, :]
 
-        def end_copy(self, k, sent):
-            if sent:
-                to = shifted(x, nx, k)
-                source, target = part.at[to, y, z, self.rows], xr.at[x, self.rows]
-            else:
-                at = shifted(x, nx, nx - k)
-                source, target = part.at[at, y, z, self.rows], xr.at[at, self.rows]
-            return sems.copy(source, target, self.end_base + k, x_peers[k - 1])
+        def end_copy(self, at, sent):
+            index = self.end_base + lax.rem(at + nx - x, nx) if sent else self.end_base + lax.rem(x + nx - at, nx)
+            target = xr.at[x if sent else at, self.rows]
+            return sems.copy(part.at[at, y, z, self.rows], target, index, device(at, y, z, c))
 
         def finish(self):
             for k in range(1, nx):
-                self.end_copy(k, False).wait_recv()
+                self.end_copy(shifted(x, nx, k), False).wait_recv()
             for source in range(2):
                 total = xr[source * hx, self.rows]
                 for k in range(1, hx):
@@ -488,12 +459,12 @@
             def one(o):
                 self.y1.sent(o)
                 self.z1.sent(o)
+                self.z2.sent(o)
                 self.y2.sent(o)
-                repeat(nz - 1, lambda k: self.z2_copy(o, k + 1, True).wait_send())
 
             repeat(nx, one)
             for k in range(1, nx):
-                self.end_copy(k, True).wait_send()
+                self.end_copy(shifted(x, nx, k), True).wait_send()
             self.fg_copy("local").wait()
             self.fg_copy("sent").wait_send()
             self.fg_copy("arrived").wait_recv()
@@ -527,35 +498,33 @@
     enc_local.wait()
     enc1.wait_recv()
     one.gathered()
+    two.gather(3)
     one.act()
-    two.gather(3)
+    two.gather(4)
     one.mask()
     one.partial()
     one.reduce(1)
-    two.gather(4)
+    two.gather_last()
     one.reduce(2)
-    two.gather_last()
     one.reduce(3)
+    two.gathered()
     one.reduce(4)
-    one.reduce(5)
-    two.gathered()
     two.act()
     two.mask()
-    one.reduce(6)
     two.partial()
     two.reduce(1)
+    one.reduce(5)
+    one.reduce(6)
+    two.reduce(2)
     one.reduce(7)
-    two.reduce(2)
-    one.reduce(8)
     two.reduce(3)
     two.reduce(4)
+    one.finish()
     two.reduce(5)
-    one.finish()
     two.reduce(6)
     two.reduce(7)
-    two.reduce(8)
+    two.finish()
     one.drain()
-    two.finish()
     two.drain()
     for copy in (dec1, enc1, pre1):
         copy.wait_send()
@@ -563,7 +532,7 @@
 
 
 def scatter_buffers(n, outer, inner, columns):
-    few = (2, outer, inner // 2, STRIP, columns) if inner > 1 else (2, outer, 1, STRIP, columns // 2)
+    few = (2, outer, inner // 2, STRIP, columns)
     full = (n // 2 - 1, 2, outer, inner, STRIP, columns)
     return [pltpu.VMEM(few, BF16)] * 2 + [pltpu.VMEM(full, BF16)] * 2
 
@@ -581,8 +550,8 @@
     bufs = [
         scatter_buffers(ny, nx, nz, ycut)
         + scatter_buffers(nz, nx, ny, width - ycut)
-        + scatter_buffers(ny, nx, 1, width - ycut)
         + [pltpu.VMEM((nx, nz, STRIP, ycut), BF16)] * 2
+        + [pltpu.VMEM((nx, ny, STRIP, width - ycut), BF16)] * 2
     ] * WAVES
     fg, ig = pl.pallas_call(
         functools.partial(kernel, (nx, ny, nz, rcut, ycut, width)),

time: 134 us -> 127 us (0.948)
  Pallas kernels: 129 us -> 122 us
    pallas_call x1, Pallas kernels: 129 us -> 122 us  [body(): pl.pallas_call(functools.partial(kernel, (nx, ny, nz, rcut, ycut, width))...]
where the time goes in v4:
time: 127 us; the launch traced here: 126 us
  Pallas kernels  122 us (96%)
  local copies, waits for them, and re-layouts  3.4 us (3%)
    pallas_call x1, Pallas kernels, body(): pl.pallas_call(functools.partial(kernel, (nx, ny, nz, rcut, ycut, width))...  122 us
    unnamed x2, local copies, waits for them, and re-layouts  3.4 us

profile of v4, /device:TPU:4, one launch (start us, length us, event | category | flops | bytes accessed | tf_op | source)
XLA Modules:
  0.0 126.0 jit_solution(14556132564551033616)
XLA Ops:
  0.6 121.9 %shard_map.77 = (bf16[16,2,32,256]{3,2,1,0:T(8,128)(2,1)}, bf16[2,32,640]{2,1,0:T(8,128)(2,1)}) custom-call(bf16[2,32,640]{2,1,0:T(8,128)(2,1)} %cot.1, bf16[256,2,5120]{2,1,0:T(2,128)(2,1)} %dec.1, bf16[5120,256]{1,0:T(8,128)(2,1)} %enc.1, bf16[16,2,32,256]{3,2,1,0:T(8,128)(2,1)} %bitcast.2, s32[2,16,32]{2,1,0:T(8,128)} %ids.1, s32[2,16]{1,0:T(2,128)} %counts.1), custom_call_target="tpu_custom_call" | custom-call | tf_op jit(solution)/shard_map/pallas_call | solution.py:556
  122.6 1.9 %copy.10 = bf16[1024,256]{1,0:T(8,128)(2,1)} copy(bf16[1024,256]{1,0:T(8,128)(2,1)} %bitcast.3) | data formatting | bytes 1048576
  124.4 1.5 %copy.11 = bf16[2,32,640]{2,1,0:T(8,128)(2,1)} copy(bf16[2,32,640]{2,1,0:T(8,128)(2,1)} %get-tuple-element.9) | data formatting | bytes 163840

commit v5 on v4

--- a/solution.py
+++ b/solution.py
@@ -299,12 +299,18 @@
             self.z1 = Scatter(
                 sems, nz, z, *z_sides, lambda i, o, js: part.at[o, js, i, rows, zhi], nx, ny, own[4:8]
             )
-            self.z2 = Exchange(
-                sems, nz, z, lambda k: (layer, shifted(z, nz, k)), lambda o, i: part.at[o, y, i, rows, ylo], nx, own[8:10]
-            )
+            if wave == 0:
+                self.z2 = Scatter(
+                    sems, nz, z, *z_sides, lambda i, o, js: part.at[js, y, i, rows, ylo], 1, nx, own[8:12]
+                )
+            else:
+                self.z2 = Exchange(
+                    sems, nz, z, lambda k: (layer, shifted(z, nz, k)), lambda o, i: part.at[o, y, i, rows, ylo], nx,
+                    own[8:10],
+                )
             self.y2 = Exchange(
                 sems, ny, y, lambda k: device(x, shifted(y, ny, k), z, c),
-                lambda o, i: part.at[o, i, z, rows, zhi], nx, own[10:12],
+                lambda o, i: part.at[o, i, z, rows, zhi], nx, own[-2:],
             )
             self.end_base = sems.take(nx)
             self.fg_base = sems.take()
@@ -345,29 +351,33 @@
 
             first_only(first)
 
-        def gathered(self):
-            all_parts(lambda n, p: self.xa.step(3, n, p))
-            first_only(lambda: all_parts(lambda n, p: self.yd.step(3, n, p)))
-
-        def act(self):
+        def act(self, *steps):
             tokens = windows * STRIP
 
-            def one(zz):
-                columns = pl.ds(pl.multiple_of(zz * width, 128), width)
-                rows1 = g1[:, :, zz, self.rows, :].reshape(tokens, width)
-                for side in range(2):
-                    term = lax.dot_general(rows1, dv[1, side, :, columns], CONTRACT, preferred_element_type=F32)
-                    acc[side] += term
+            def term(target, side, at):
+                ref = g1 if target else g0
+                rows = ref[:, :, at, self.rows, :].reshape(tokens, width)
+                columns = pl.ds(pl.multiple_of(at * width, 128), width)
+                return lax.dot_general(rows, dv[target, side, :, columns], CONTRACT, preferred_element_type=F32)
+
+            def one(number, at):
+                self.xa.step(3, number, at)
 
                 @pl.when(is_first)
                 def _():
-                    rows0 = g0[:, :, zz, self.rows, :].reshape(tokens, width)
+                    self.yd.step(3, number, at)
                     for side in range(2):
-                        term = lax.dot_general(rows0, dv[0, side, :, columns], CONTRACT, preferred_element_type=F32)
-                        acc[side] += term
-
-            acc[...] = jnp.zeros_like(acc)
-            repeat(nz, one)
+                        acc[side] += term(1, side, at) + term(0, side, at)
+
+                @pl.when(jnp.logical_not(is_first))
+                def _():
+                    for side in range(2):
+                        acc[side] += term(1, side, at)
+
+            for step in steps:
+                if step == 0:
+                    acc[...] = jnp.zeros_like(acc)
+                each_part(step, one)
 
         def mask(self):
             def one(w):
@@ -410,9 +420,12 @@
             elif stage == 5:
                 def one(o):
                     self.y1.final(o)
-                    self.z2.start(o)
+                    if self.wave == 1:
+                        self.z2.start(o)
 
                 repeat(nx, one)
+                if self.wave == 0:
+                    self.z2.step(1, 0)
             elif stage == 6:
                 def one(o):
                     self.z1.final(o)
@@ -420,8 +433,12 @@
 
                 repeat(nx, one)
             else:
+                if self.wave == 0:
+                    self.z2.final(0)
+
                 def one(o):
-                    self.z2.final(o)
+                    if self.wave == 1:
+                        self.z2.final(o)
                     self.y2.final(o)
                     pl.when(o != x)(lambda: self.end_copy(o, True).start())
 
@@ -459,10 +476,13 @@
             def one(o):
                 self.y1.sent(o)
                 self.z1.sent(o)
-                self.z2.sent(o)
                 self.y2.sent(o)
+                if self.wave == 1:
+                    self.z2.sent(o)
 
             repeat(nx, one)
+            if self.wave == 0:
+                self.z2.sent(0)
             for k in range(1, nx):
                 self.end_copy(shifted(x, nx, k), True).wait_send()
             self.fg_copy("local").wait()
@@ -497,31 +517,35 @@
     pre1.wait_recv()
     enc_local.wait()
     enc1.wait_recv()
-    one.gathered()
+    one.act(0, 1, 2)
     two.gather(3)
-    one.act()
+    one.act(3, 4)
     two.gather(4)
     one.mask()
     one.partial()
     one.reduce(1)
     two.gather_last()
+    two.act(0, 1)
     one.reduce(2)
+    two.act(2, 3)
     one.reduce(3)
-    two.gathered()
+    two.act(4)
+    two.mask()
     one.reduce(4)
-    two.act()
-    two.mask()
     two.partial()
     two.reduce(1)
     one.reduce(5)
+    two.reduce(2)
     one.reduce(6)
-    two.reduce(2)
+    one.z2.step(2, 0)
+    two.reduce(3)
+    one.z2.step(3, 0)
+    two.reduce(4)
+    one.z2.step(4, 0)
+    two.reduce(5)
     one.reduce(7)
-    two.reduce(3)
-    two.reduce(4)
+    two.reduce(6)
     one.finish()
-    two.reduce(5)
-    two.reduce(6)
     two.reduce(7)
     two.finish()
     one.drain()
@@ -547,12 +571,12 @@
     any_ref = pl.BlockSpec(memory_space=pl.ANY)
     vmem_ref = pl.BlockSpec(memory_space=pltpu.VMEM)
     pieces = (nx, ny, nz, ROWS, width)
+    common = scatter_buffers(ny, nx, nz, ycut) + scatter_buffers(nz, nx, ny, width - ycut)
+    last = [pltpu.VMEM((nx, ny, STRIP, width - ycut), BF16)] * 2
     bufs = [
-        scatter_buffers(ny, nx, nz, ycut)
-        + scatter_buffers(nz, nx, ny, width - ycut)
-        + [pltpu.VMEM((nx, nz, STRIP, ycut), BF16)] * 2
-        + [pltpu.VMEM((nx, ny, STRIP, width - ycut), BF16)] * 2
-    ] * WAVES
+        common + scatter_buffers(nz, 1, nx, ycut) + last,
+        common + [pltpu.VMEM((nx, nz, STRIP, ycut), BF16)] * 2 + last,
+    ]
     fg, ig = pl.pallas_call(
         functools.partial(kernel, (nx, ny, nz, rcut, ycut, width)),
         out_shape=(

time: 127 us -> 120 us (0.945)
  Pallas kernels: 122 us -> 115 us
    pallas_call x1, Pallas kernels: 122 us -> 115 us  [body(): pl.pallas_call(functools.partial(kernel, (nx, ny, nz, rcut, ycut, width))...]
where the time goes in v5:
time: 120 us; the launch traced here: 119 us
  Pallas kernels  115 us (96%)
  local copies, waits for them, and re-layouts  3.4 us (3%)
    pallas_call x1, Pallas kernels, body(): pl.pallas_call(functools.partial(kernel, (nx, ny, nz, rcut, ycut, width))...  115 us
    unnamed x2, local copies, waits for them, and re-layouts  3.4 us

profile of v5, /device:TPU:4, one launch (start us, length us, event | category | flops | bytes accessed | tf_op | source)
XLA Modules:
  0.0 118.8 jit_solution(17746656005342320295)
XLA Ops:
  0.6 114.7 %shard_map.77 = (bf16[16,2,32,256]{3,2,1,0:T(8,128)(2,1)}, bf16[2,32,640]{2,1,0:T(8,128)(2,1)}) custom-call(bf16[2,32,640]{2,1,0:T(8,128)(2,1)} %cot.1, bf16[256,2,5120]{2,1,0:T(2,128)(2,1)} %dec.1, bf16[5120,256]{1,0:T(8,128)(2,1)} %enc.1, bf16[16,2,32,256]{3,2,1,0:T(8,128)(2,1)} %bitcast.2, s32[2,16,32]{2,1,0:T(8,128)} %ids.1, s32[2,16]{1,0:T(2,128)} %counts.1), custom_call_target="tpu_custom_call" | custom-call | tf_op jit(solution)/shard_map/pallas_call | solution.py:580
  115.4 1.9 %copy.10 = bf16[1024,256]{1,0:T(8,128)(2,1)} copy(bf16[1024,256]{1,0:T(8,128)(2,1)} %bitcast.3) | data formatting | bytes 1048576
  117.2 1.5 %copy.11 = bf16[2,32,640]{2,1,0:T(8,128)(2,1)} copy(bf16[2,32,640]{2,1,0:T(8,128)(2,1)} %get-tuple-element.9) | data formatting | bytes 163840

commit v6 on v5

--- a/solution.py
+++ b/solution.py
@@ -192,7 +192,7 @@
 def kernel(
     dims, cot, dec, enc, pre, ids, counts, fg_out, ig_out, g0, g1, raw, dv, ev, pv, fg, hit, acc, part, xr, bufs, send, recv, local
 ):
-    nx, ny, nz, rcut, ycut, width = dims
+    nx, ny, nz, rcut, ycut, zcut, width = dims
     hx = nx // 2
     windows, feats = nx * ny, dv.shape[2]
     layer = lax.axis_index("layer")
@@ -236,7 +236,9 @@
 
     sems = Semaphores(send, recv)
     rlo, rhi = pl.ds(0, rcut), pl.ds(rcut, width - rcut)
-    ylo, zhi = pl.ds(0, ycut), pl.ds(ycut, width - ycut)
+    ylo, xmid, zhi = pl.ds(0, ycut), pl.ds(ycut, zcut - ycut), pl.ds(zcut, width - zcut)
+    partner = device(x + 1 - 2 * lax.rem(x, 2), y, z, c)
+    mine, others = lax.rem(x, 2) * hx, (1 - lax.rem(x, 2)) * hx
 
     dec1 = sems.copy(dv.at[1, c], dv.at[1, c], sems.take(), sibling)
     dec0 = sems.copy(dv.at[0, c], dv.at[0, c], sems.take(), sibling)
@@ -312,6 +314,15 @@
                 sems, ny, y, lambda k: device(x, shifted(y, ny, k), z, c),
                 lambda o, i: part.at[o, i, z, rows, zhi], nx, own[-2:],
             )
+            self.pair_send, self.pair_recv = own[-4:-2]
+            self.pair_base = sems.take(hx)
+            self.y3 = Scatter(
+                sems, ny, y, *y_sides, lambda i, o, js: part.at[mine + o, i, js, rows, xmid], hx, nz, own[-8:-4]
+            )
+            self.z3 = Exchange(
+                sems, nz, z, lambda k: (layer, shifted(z, nz, k)), lambda o, i: part.at[mine + o, y, i, rows, xmid], hx,
+                own[-10:-8],
+            )
             self.end_base = sems.take(nx)
             self.fg_base = sems.take()
 
@@ -412,11 +423,31 @@
 
             repeat(nz, one)
 
+        def pair_copy(self, o):
+            return sems.copy(self.pair_send.at[o], self.pair_recv.at[o], self.pair_base + o, partner)
+
+        def pair_start(self, o):
+            self.pair_send[o] = part[others + o, :, :, self.rows, xmid].astype(BF16)
+            self.pair_copy(o).start()
+
+        def pair_final(self, o):
+            self.pair_copy(o).wait_recv()
+            part[mine + o, :, :, self.rows, xmid] = (
+                part[mine + o, :, :, self.rows, xmid] + self.pair_recv[o].astype(F32)
+            )
+            self.y3.step(1, o)
+
         def reduce(self, stage):
+            if stage == 1:
+                repeat(hx, self.pair_start)
             if stage <= nz // 2:
                 repeat(nx, lambda o: self.z1.step(stage, o))
                 if stage <= ny // 2:
                     repeat(nx, lambda o: self.y1.step(stage, o))
+                elif stage == 3:
+                    repeat(hx, self.pair_final)
+                else:
+                    repeat(hx, lambda o: self.y3.step(2, o))
             elif stage == 5:
                 def one(o):
                     self.y1.final(o)
@@ -427,12 +458,18 @@
                 if self.wave == 0:
                     self.z2.step(1, 0)
             elif stage == 6:
+                def third(o):
+                    self.y3.final(o)
+                    self.z3.start(o)
+
                 def one(o):
                     self.z1.final(o)
                     self.y2.start(o)
 
+                repeat(hx, third)
                 repeat(nx, one)
             else:
+                repeat(hx, self.z3.final)
                 if self.wave == 0:
                     self.z2.final(0)
 
@@ -458,6 +495,7 @@
                 for k in range(1, hx):
                     total = total + xr[source * hx + k, self.rows]
                 ig_out[source, self.rows] = total.astype(BF16)
+                ig_out[source, self.rows, xmid] = xr[source * hx + x // hx, self.rows, xmid].astype(BF16)
 
         def drain(self):
             self.ya.sent()
@@ -480,7 +518,13 @@
                 if self.wave == 1:
                     self.z2.sent(o)
 
+            def pair(o):
+                self.pair_copy(o).wait_send()
+                self.y3.sent(o)
+                self.z3.sent(o)
+
             repeat(nx, one)
+            repeat(hx, pair)
             if self.wave == 0:
                 self.z2.sent(0)
             for k in range(1, nx):
@@ -495,22 +539,22 @@
         copy.start()
     find_blocks()
     one.gather(0)
+    two.begin()
     dec_local.wait()
     sort_targets(0)
     one.gather(1)
     sort_targets(1)
     one.gather(2)
-    two.begin()
+    two.gather(0)
     sort_targets(2)
     one.gather(3)
-    two.gather(0)
+    two.gather(1)
     sort_targets(3)
     dec1.start()
     first_only(dec0.start)
     one.gather(4)
-    two.gather(1)
+    two.gather(2)
     one.gather_last()
-    two.gather(2)
     dec1.wait_recv()
     first_only(dec0.wait_recv)
     pre_local.wait()
@@ -567,18 +611,24 @@
     num_layers = decoder.shape[1]
     feats, width = decoder.shape[0], cotangent.shape[2]
     windows = preact.shape[0] // WIN
-    rcut, ycut = width - 128, width - 256
+    rcut, ycut, zcut = width - 128, width - 384, width - 256
     any_ref = pl.BlockSpec(memory_space=pl.ANY)
     vmem_ref = pl.BlockSpec(memory_space=pltpu.VMEM)
     pieces = (nx, ny, nz, ROWS, width)
-    common = scatter_buffers(ny, nx, nz, ycut) + scatter_buffers(nz, nx, ny, width - ycut)
-    last = [pltpu.VMEM((nx, ny, STRIP, width - ycut), BF16)] * 2
+    common = scatter_buffers(ny, nx, nz, ycut) + scatter_buffers(nz, nx, ny, width - zcut)
+    hx, middle = nx // 2, zcut - ycut
+    last = (
+        [pltpu.VMEM((hx, nz, STRIP, middle), BF16)] * 2
+        + scatter_buffers(ny, hx, nz, middle)
+        + [pltpu.VMEM((hx, ny, nz, STRIP, middle), BF16)] * 2
+        + [pltpu.VMEM((nx, ny, STRIP, width - zcut), BF16)] * 2
+    )
     bufs = [
         common + scatter_buffers(nz, 1, nx, ycut) + last,
         common + [pltpu.VMEM((nx, nz, STRIP, ycut), BF16)] * 2 + last,
     ]
     fg, ig = pl.pallas_call(
-        functools.partial(kernel, (nx, ny, nz, rcut, ycut, width)),
+        functools.partial(kernel, (nx, ny, nz, rcut, ycut, zcut, width)),
         out_shape=(
             jax.ShapeDtypeStruct((windows, 2, ROWS, feats), BF16),
             jax.ShapeDtypeStruct((num_layers, ROWS, width), BF16),
@@ -598,8 +648,8 @@
             pltpu.VMEM(pieces, F32),
             pltpu.VMEM((nx, ROWS, width), F32),
             bufs,
-            pltpu.SemaphoreType.DMA((512,)),
-            pltpu.SemaphoreType.DMA((512,)),
+            pltpu.SemaphoreType.DMA((560,)),
+            pltpu.SemaphoreType.DMA((560,)),
             pltpu.SemaphoreType.DMA((5 + WAVES,)),
         ],
         compiler_params=pltpu.CompilerParams(

time: 120 us -> 120 us (level)
  no operation moved by 1% of the time
where the time goes in v6:
time: 120 us
  Pallas kernels  116 us (97%)
  local copies, waits for them, and re-layouts  3.4 us (3%)
    pallas_call x1, Pallas kernels, body(): pl.pallas_call(functools.partial(kernel, (nx, ny, nz, rcut, ycut, zcut, w...  116 us
    unnamed x2, local copies, waits for them, and re-layouts  3.4 us

profile of v6, /device:TPU:4, one launch (start us, length us, event | category | flops | bytes accessed | tf_op | source)
XLA Modules:
  0.0 119.8 jit_solution(9444190135877795538)
XLA Ops:
  0.6 115.8 %shard_map.77 = (bf16[16,2,32,256]{3,2,1,0:T(8,128)(2,1)}, bf16[2,32,640]{2,1,0:T(8,128)(2,1)}) custom-call(bf16[2,32,640]{2,1,0:T(8,128)(2,1)} %cot.1, bf16[256,2,5120]{2,1,0:T(2,128)(2,1)} %dec.1, bf16[5120,256]{1,0:T(8,128)(2,1)} %enc.1, bf16[16,2,32,256]{3,2,1,0:T(8,128)(2,1)} %bitcast.2, s32[2,16,32]{2,1,0:T(8,128)} %ids.1, s32[2,16]{1,0:T(2,128)} %counts.1), custom_call_target="tpu_custom_call" | custom-call | tf_op jit(solution)/shard_map/pallas_call | solution.py:630
  116.4 1.9 %copy.10 = bf16[1024,256]{1,0:T(8,128)(2,1)} copy(bf16[1024,256]{1,0:T(8,128)(2,1)} %bitcast.3) | data formatting | bytes 1048576
  118.3 1.5 %copy.11 = bf16[2,32,640]{2,1,0:T(8,128)(2,1)} copy(bf16[2,32,640]{2,1,0:T(8,128)(2,1)} %get-tuple-element.9) | data formatting | bytes 163840

commit v7 on v5

--- a/solution.py
+++ b/solution.py
@@ -459,7 +459,7 @@
                     total = total + xr[source * hx + k, self.rows]
                 ig_out[source, self.rows] = total.astype(BF16)
 
-        def drain(self):
+        def gather_sent(self):
             self.ya.sent()
             self.xt.sent()
             self.za.sent()
@@ -472,22 +472,25 @@
                 all_parts(self.yd.sent)
 
             first_only(first)
-
+            self.fg_copy("local").wait()
+            self.fg_copy("sent").wait_send()
+            self.fg_copy("arrived").wait_recv()
+
+        def rings_sent(self):
             def one(o):
                 self.y1.sent(o)
                 self.z1.sent(o)
-                self.y2.sent(o)
-                if self.wave == 1:
-                    self.z2.sent(o)
 
             repeat(nx, one)
+
+        def rest_sent(self):
+            repeat(nx, self.y2.sent)
             if self.wave == 0:
                 self.z2.sent(0)
+            else:
+                repeat(nx, self.z2.sent)
             for k in range(1, nx):
                 self.end_copy(shifted(x, nx, k), True).wait_send()
-            self.fg_copy("local").wait()
-            self.fg_copy("sent").wait_send()
-            self.fg_copy("arrived").wait_recv()
 
     one, two = Wave(0), Wave(1)
     one.begin()
@@ -495,22 +498,22 @@
         copy.start()
     find_blocks()
     one.gather(0)
+    two.begin()
     dec_local.wait()
     sort_targets(0)
     one.gather(1)
     sort_targets(1)
     one.gather(2)
-    two.begin()
+    two.gather(0)
     sort_targets(2)
     one.gather(3)
-    two.gather(0)
+    two.gather(1)
     sort_targets(3)
     dec1.start()
     first_only(dec0.start)
     one.gather(4)
-    two.gather(1)
+    two.gather(2)
     one.gather_last()
-    two.gather(2)
     dec1.wait_recv()
     first_only(dec0.wait_recv)
     pre_local.wait()
@@ -534,6 +537,7 @@
     one.reduce(4)
     two.partial()
     two.reduce(1)
+    one.gather_sent()
     one.reduce(5)
     two.reduce(2)
     one.reduce(6)
@@ -541,15 +545,18 @@
     two.reduce(3)
     one.z2.step(3, 0)
     two.reduce(4)
+    two.gather_sent()
     one.z2.step(4, 0)
     two.reduce(5)
     one.reduce(7)
     two.reduce(6)
     one.finish()
+    one.rings_sent()
+    two.rings_sent()
     two.reduce(7)
     two.finish()
-    one.drain()
-    two.drain()
+    one.rest_sent()
+    two.rest_sent()
     for copy in (dec1, enc1, pre1):
         copy.wait_send()
     first_only(dec0.wait_send)

time: 120 us -> 119 us (level)
  Pallas kernels: 115 us -> 113 us
    pallas_call x1, Pallas kernels: 115 us -> 113 us  [body(): pl.pallas_call(functools.partial(kernel, (nx, ny, nz, rcut, ycut, width))...]
where the time goes in v7:
time: 119 us; the launch traced here: 117 us
  Pallas kernels  113 us (95%)
  local copies, waits for them, and re-layouts  3.4 us (3%)
    pallas_call x1, Pallas kernels, body(): pl.pallas_call(functools.partial(kernel, (nx, ny, nz, rcut, ycut, width))...  113 us
    unnamed x2, local copies, waits for them, and re-layouts  3.4 us

profile of v7, /device:TPU:4, one launch (start us, length us, event | category | flops | bytes accessed | tf_op | source)
XLA Modules:
  0.0 117.3 jit_solution(5684381737420441454)
XLA Ops:
  0.6 113.3 %shard_map.77 = (bf16[16,2,32,256]{3,2,1,0:T(8,128)(2,1)}, bf16[2,32,640]{2,1,0:T(8,128)(2,1)}) custom-call(bf16[2,32,640]{2,1,0:T(8,128)(2,1)} %cot.1, bf16[256,2,5120]{2,1,0:T(2,128)(2,1)} %dec.1, bf16[5120,256]{1,0:T(8,128)(2,1)} %enc.1, bf16[16,2,32,256]{3,2,1,0:T(8,128)(2,1)} %bitcast.2, s32[2,16,32]{2,1,0:T(8,128)} %ids.1, s32[2,16]{1,0:T(2,128)} %counts.1), custom_call_target="tpu_custom_call" | custom-call | tf_op jit(solution)/shard_map/pallas_call | solution.py:587
  113.9 1.9 %copy.10 = bf16[1024,256]{1,0:T(8,128)(2,1)} copy(bf16[1024,256]{1,0:T(8,128)(2,1)} %bitcast.3) | data formatting | bytes 1048576
  115.8 1.5 %copy.11 = bf16[2,32,640]{2,1,0:T(8,128)(2,1)} copy(bf16[2,32,640]{2,1,0:T(8,128)(2,1)} %get-tuple-element.9) | data formatting | bytes 163840
